TPU v7x, 32 devices: a whole 2x2x4 slice. The times are simulated.
32 devices in a mesh: dp: 4 (over x, core), row: 4 (over z), col: 2 (over y).
Axes of the slice: x: 2, y: 2, z: 4, core: 2. Of those that a mesh axis runs over, the one named last changes fastest.
Arguments:
- tokens: float32 [6304, 1024], P('dp', ('row', 'col')), may hold values from -6 to 6
- cotangent: float32 [6304, 1024], P('dp', ('row', 'col')), may hold values from -6 to 6
- w_qkv: bfloat16 [1024, 3, 16, 64], P('row', None, 'col', 'dp'), may hold values from -0.4375 to 0.4375
- b_qkv: bfloat16 [2, 16, 64], P(None, 'col', 'dp'), may hold values from -3 to 3
- w_out: bfloat16 [16, 64, 1024], P('col', 'dp', 'row'), may hold values from -1 to 1
- w_up: bfloat16 [1024, 64, 64], P('row', 'col', 'dp'), may hold values from -0.34375 to 0.34375
- b_up: bfloat16 [64, 64], P('col', 'dp'), may hold values from -3 to 3
- w_down: bfloat16 [64, 64, 1024], P('col', 'dp', 'row'), may hold values from -0.09375 to 0.09375
- vectors: bfloat16 [6, 16, 64], P(None, ('row', 'col'), 'dp'), may hold values from -1.2 to 1.4, as said below
- state_qkv: float32 [2, 1024, 3, 16, 64], P(None, 'row', None, 'col', 'dp'), may hold values from -4.5 to 4.5, as said below
- state_qkv_bias: float32 [2, 2, 16, 64], P(None, None, 'col', 'dp'), may hold values from -4.5 to 4.5, as said below
- state_out: float32 [2, 16, 64, 1024], P(None, 'col', 'dp', 'row'), may hold values from -14.5 to 14.5, as said below
- state_up: float32 [2, 1024, 64, 64], P(None, 'row', 'col', 'dp'), may hold values from -3.9 to 3.9, as said below
- state_up_bias: float32 [2, 64, 64], P(None, 'col', 'dp'), may hold values from -3.9 to 3.9, as said below
- state_down: float32 [2, 64, 64, 1024], P(None, 'col', 'dp', 'row'), may hold values from -7.4 to 7.4, as said below
- state_vectors: float32 [2, 6, 16, 64], P(None, None, ('row', 'col'), 'dp'), may hold values from -14.5 to 14.5, as said below
Outputs:
- layer_out: float32 [6304, 1024], P('dp', ('row', 'col'))
- grad_tokens: float32 [6304, 1024], P('dp', ('row', 'col'))
- grad_w_qkv: float32 [1024, 3, 16, 64], P('row', None, 'col', 'dp')
- grad_b_qkv: float32 [2, 16, 64], P(None, 'col', 'dp')
- grad_w_out: float32 [16, 64, 1024], P('col', 'dp', 'row')
- grad_w_up: float32 [1024, 64, 64], P('row', 'col', 'dp')
- grad_b_up: float32 [64, 64], P('col', 'dp')
- grad_w_down: float32 [64, 64, 1024], P('col', 'dp', 'row')
- grad_vectors: float32 [6, 16, 64], P(None, ('row', 'col'), 'dp')
- change_w_qkv: float32 [1024, 3, 16, 64], P('row', None, 'col', 'dp')
- change_b_qkv: float32 [2, 16, 64], P(None, 'col', 'dp')
- change_w_out: float32 [16, 64, 1024], P('col', 'dp', 'row')
- change_w_up: float32 [1024, 64, 64], P('row', 'col', 'dp')
- change_b_up: float32 [64, 64], P('col', 'dp')
- change_w_down: float32 [64, 64, 1024], P('col', 'dp', 'row')
- change_vectors: float32 [6, 16, 64], P(None, ('row', 'col'), 'dp')
- new_state_qkv: float32 [2, 1024, 3, 16, 64], P(None, 'row', None, 'col', 'dp')
- new_state_qkv_bias: float32 [2, 2, 16, 64], P(None, None, 'col', 'dp')
- new_state_out: float32 [2, 16, 64, 1024], P(None, 'col', 'dp', 'row')
- new_state_up: float32 [2, 1024, 64, 64], P(None, 'row', 'col', 'dp')
- new_state_up_bias: float32 [2, 64, 64], P(None, 'col', 'dp')
- new_state_down: float32 [2, 64, 64, 1024], P(None, 'col', 'dp', 'row')
- new_state_vectors: float32 [2, 6, 16, 64], P(None, None, ('row', 'col'), 'dp')
Inputs may be any that keep to these rules, and one draw needn't show every extreme that they name: `vectors`: rows 0 and 3 are gains between 0.6 and 1.4. `state_qkv`: slice 0 is the first moment; slice 1, the second moment, is positive. `state_qkv_bias`: slice 0 is the first moment; slice 1, the second moment, is positive. `state_out`: slice 0 is the first moment; slice 1, the second moment, is positive. `state_up`: slice 0 is the first moment; slice 1, the second moment, is positive. `state_up_bias`: slice 0 is the first moment; slice 1, the second moment, is positive. `state_down`: slice 0 is the first moment; slice 1, the second moment, is positive. `state_vectors`: slice 0 is the first moment; slice 1, the second moment, is positive.
All inputs are finite; a program needn't handle non-finite values.
Results may differ from a plain program's by a relative error of at most 0.023.
Values may be sent and summed in bfloat16 or wider, within the bound.
No kernel may reach another device: no remote copies, remote signals or barrier semaphores. Data moves between devices by JAX's collectives and lax.ppermute only.
A program may use at most 128 MiB of HBM per device.

v0:
```python
import math

import jax
import jax.numpy as jnp
from jax import lax
from jax.sharding import PartitionSpec as P

HD = 64
SEQ = 197
STEP = 10


norm_eps = 1e-06
beta_first = 0.9
beta_second = 0.999
learn_rate = 0.01
weight_decay = 0.05
adam_eps = 1e-08
grad_gain = 32.0


def exact_gelu(values):
    return jax.nn.gelu(values, approximate=False)


def norm_forward(stream, norm_gain, norm_shift):
    feature_width = stream.shape[1] * lax.axis_size(("row", "col"))
    totals = lax.psum((jnp.sum(stream, axis=1), jnp.sum(stream * stream, axis=1)), ("row", "col"))
    center = totals[0] / feature_width
    spread = totals[1] / feature_width - center * center
    inv_std = lax.rsqrt(spread + norm_eps)[:, None]
    scaled = (stream - center[:, None]) * inv_std
    return ((scaled * norm_gain + norm_shift).astype(jnp.bfloat16), scaled, inv_std)


def norm_backward(grad_norm, scaled, inv_std, norm_gain):
    feature_width = grad_norm.shape[1] * lax.axis_size(("row", "col"))
    weighted = grad_norm * norm_gain
    totals = lax.psum(
        (jnp.sum(weighted, axis=1), jnp.sum(weighted * scaled, axis=1)), ("row", "col")
    )
    grad_input = inv_std * (
        weighted - totals[0][:, None] / feature_width - scaled * totals[1][:, None] / feature_width
    )
    return (grad_input, jnp.sum(grad_norm * scaled, axis=0), jnp.sum(grad_norm, axis=0))


def col_pieces(values):
    return lax.all_gather(values, "col", axis=1, tiled=True)


def col_total(partial_value):
    return lax.psum_scatter(partial_value, "col", scatter_dimension=1, tiled=True)


def project_in(normed, weight_flat, groups):
    gathered = col_pieces(normed)
    partial_value = jnp.dot(gathered, weight_flat, preferred_element_type=jnp.float32)
    partial_value = partial_value.reshape(partial_value.shape[0], groups, -1)
    return (gathered, lax.psum_scatter(partial_value, "row", scatter_dimension=2, tiled=True))


def project_out(mixed, weight_flat):
    gathered = lax.all_gather(mixed, "row", axis=1, tiled=True)
    partial_value = jnp.dot(gathered, weight_flat, preferred_element_type=jnp.float32)
    return (gathered, col_total(partial_value))


def back_out(grad_low, kept_input, weight_flat):
    grad_rows = col_pieces(grad_low)
    weight_grad = jnp.einsum("tf,td->fd", kept_input, grad_rows, preferred_element_type=jnp.float32)
    partial_value = jnp.einsum(
        "td,fd->tf", grad_rows, weight_flat, preferred_element_type=jnp.float32
    )
    partial_value = partial_value.reshape(partial_value.shape[0], 1, -1)
    return (
        weight_grad,
        lax.psum_scatter(partial_value, "row", scatter_dimension=2, tiled=True)[:, 0],
    )


def back_in(grad_low, kept_input, weight_flat):
    grad_cols = lax.all_gather(grad_low, "row", axis=2, tiled=True)
    grad_flat = grad_cols.reshape(grad_cols.shape[0], -1)
    weight_grad = jnp.einsum("td,tf->df", kept_input, grad_flat, preferred_element_type=jnp.float32)
    bias_grad = jnp.sum(grad_cols, axis=0, dtype=jnp.float32)
    partial_value = jnp.einsum(
        "tf,df->td", grad_flat, weight_flat, preferred_element_type=jnp.float32
    )
    return (weight_grad, bias_grad, col_total(partial_value))


def split_packed(packed_low):
    images = packed_low.shape[0] // SEQ
    head_count = packed_low.shape[2] // HD
    return packed_low.reshape(images, SEQ, 3, head_count, HD)


def attend(packed_low):
    split_heads = split_packed(packed_low)
    scores = jnp.einsum(
        "nqhe,nkhe->nhqk",
        split_heads[:, :, 0],
        split_heads[:, :, 1],
        preferred_element_type=jnp.float32,
    ) * (1.0 / math.sqrt(HD))
    row_max = jnp.max(scores, axis=-1, keepdims=True)
    log_total = row_max + jnp.log(jnp.sum(jnp.exp(scores - row_max), axis=-1, keepdims=True))
    weights = jnp.exp(scores - log_total).astype(jnp.bfloat16)
    attended = jnp.einsum(
        "nhqk,nkhe->nqhe", weights, split_heads[:, :, 2], preferred_element_type=jnp.float32
    )
    return (attended.reshape(packed_low.shape[0], -1), log_total)


def attend_back(packed_low, log_total, grad_low):
    split_heads = split_packed(packed_low)
    queries = split_heads[:, :, 0]
    key_rows = split_heads[:, :, 1]
    values = split_heads[:, :, 2]
    score_scale = 1.0 / math.sqrt(HD)
    scores = (
        jnp.einsum("nqhe,nkhe->nhqk", queries, key_rows, preferred_element_type=jnp.float32)
        * score_scale
    )
    weights = jnp.exp(scores - log_total)
    grad_heads = grad_low.reshape(queries.shape)
    grad_values = jnp.einsum(
        "nhqk,nqhe->nkhe",
        weights.astype(jnp.bfloat16),
        grad_heads,
        preferred_element_type=jnp.float32,
    )
    grad_weights = jnp.einsum(
        "nqhe,nkhe->nhqk", grad_heads, values, preferred_element_type=jnp.float32
    )
    grad_scores = weights * (grad_weights - jnp.sum(grad_weights * weights, axis=-1, keepdims=True))
    grad_scores = grad_scores.astype(jnp.bfloat16)
    grad_queries = (
        jnp.einsum("nhqk,nkhe->nqhe", grad_scores, key_rows, preferred_element_type=jnp.float32)
        * score_scale
    )
    grad_keys = (
        jnp.einsum("nhqk,nqhe->nkhe", grad_scores, queries, preferred_element_type=jnp.float32)
        * score_scale
    )
    stacked = jnp.stack([grad_queries, grad_keys, grad_values], axis=2)
    return stacked.reshape(packed_low.shape[0], 3, -1).astype(jnp.bfloat16)


def adam_step(weight_old, gradient, moments, decay_on):
    first_moment = beta_first * moments[0] + (1.0 - beta_first) * gradient
    second_moment = beta_second * moments[1] + (1.0 - beta_second) * gradient * gradient
    first_hat = first_moment / (1.0 - beta_first**STEP)
    second_hat = second_moment / (1.0 - beta_second**STEP)
    change = -learn_rate * (first_hat / (jnp.sqrt(second_hat) + adam_eps) + decay_on * weight_old)
    return (change, jnp.stack([first_moment, second_moment]))


def on_device(
    tokens,
    cotangent,
    w_qkv,
    b_qkv,
    w_out,
    w_up,
    b_up,
    w_down,
    vectors,
    state_qkv,
    state_qkv_bias,
    state_out,
    state_up,
    state_up_bias,
    state_down,
    state_vectors,
):
    gathered_params = (
        lax.all_gather(w_qkv, "dp", axis=3, tiled=True),
        lax.all_gather(b_qkv, "dp", axis=2, tiled=True),
        lax.all_gather(w_out, "dp", axis=1, tiled=True),
        lax.all_gather(w_up, "dp", axis=2, tiled=True),
        lax.all_gather(b_up, "dp", axis=1, tiled=True),
        lax.all_gather(w_down, "dp", axis=1, tiled=True),
        lax.all_gather(vectors, "dp", axis=2, tiled=True),
    )
    qkv_block, bias_block, out_block, up_block, unit_bias, down_block, vector_block = (
        gathered_params
    )
    row_index = lax.axis_index("row")
    row_count = lax.axis_size("row")
    vector_rows = vector_block.reshape(6, -1).astype(jnp.float32)
    qkv_use, out_use, up_use, down_use = (qkv_block, out_block, up_block, down_block)
    block_flat = qkv_block.reshape(qkv_block.shape[0], -1)
    head_width = block_flat.shape[1] // (3 * row_count)
    bias_rows = lax.dynamic_slice_in_dim(
        bias_block.reshape(2, -1), row_index * head_width, head_width, 1
    ).astype(jnp.float32)
    unit_width = up_block.reshape(up_block.shape[0], -1).shape[1] // row_count
    unit_rows = lax.dynamic_slice_in_dim(
        unit_bias.reshape(-1), row_index * unit_width, unit_width, 0
    ).astype(jnp.float32)
    qkv_flat = qkv_use.reshape(qkv_use.shape[0], -1)
    out_flat = out_use.reshape(-1, out_use.shape[2])
    up_flat = up_use.reshape(up_use.shape[0], -1)
    down_flat = down_use.reshape(-1, down_use.shape[2])
    normed_one, scaled_one, inv_one = norm_forward(tokens, vector_rows[0], vector_rows[1])
    kept_one, packed = project_in(normed_one, qkv_flat, 3)
    packed = packed + jnp.stack([bias_rows[0], jnp.zeros_like(bias_rows[0]), bias_rows[1]])[None]
    packed_low = packed.astype(jnp.bfloat16)
    attended, log_total = attend(packed_low)
    heads_low = attended.astype(jnp.bfloat16)
    kept_heads, branch = project_out(heads_low, out_flat)
    middle = tokens + (branch + vector_rows[2])
    normed_two, scaled_two, inv_two = norm_forward(middle, vector_rows[3], vector_rows[4])
    kept_two, hidden = project_in(normed_two, up_flat, 1)
    hidden = hidden[:, 0]
    hidden = hidden + unit_rows
    activated, gelu_pull = jax.vjp(exact_gelu, hidden)
    units_low = activated.astype(jnp.bfloat16)
    kept_units, mixed = project_out(units_low, down_flat)
    result = middle + (mixed + vector_rows[5])
    grad_top = cotangent.astype(jnp.bfloat16)
    down_grad, grad_units = back_out(grad_top, kept_units, down_flat)
    grad_hidden = gelu_pull(grad_units)[0].astype(jnp.bfloat16)
    up_grad, unit_grad, grad_normed_two = back_in(grad_hidden[:, None], kept_two, up_flat)
    norm_grad_two, gain_two_grad, shift_two_grad = norm_backward(
        grad_normed_two, scaled_two, inv_two, vector_rows[3]
    )
    grad_middle = cotangent + norm_grad_two
    grad_branch = grad_middle.astype(jnp.bfloat16)
    out_grad, grad_heads = back_out(grad_branch, kept_heads, out_flat)
    grad_packed = attend_back(packed_low, log_total, grad_heads.astype(jnp.bfloat16))
    qkv_grad, packed_bias_grad, grad_normed_one = back_in(grad_packed, kept_one, qkv_flat)
    norm_grad_one, gain_one_grad, shift_one_grad = norm_backward(
        grad_normed_one, scaled_one, inv_one, vector_rows[0]
    )
    grad_tokens = grad_middle + norm_grad_one
    vector_grad = jnp.stack(
        [
            gain_one_grad,
            shift_one_grad,
            jnp.sum(grad_branch, axis=0, dtype=jnp.float32),
            gain_two_grad,
            shift_two_grad,
            jnp.sum(grad_top, axis=0, dtype=jnp.float32),
        ]
    ).reshape(vector_block.shape)
    query_value_grad = jnp.stack([packed_bias_grad[0], packed_bias_grad[2]]).reshape(
        bias_block.shape
    )
    unit_grad = unit_grad.reshape(unit_bias.shape)
    local_grads = (
        qkv_grad.reshape(qkv_block.shape),
        query_value_grad,
        out_grad.reshape(out_block.shape),
        up_grad.reshape(up_block.shape),
        unit_grad,
        down_grad.reshape(down_block.shape),
    )
    summed = (
        lax.psum_scatter(local_grads[0], "dp", scatter_dimension=3, tiled=True),
        lax.psum_scatter(local_grads[1], "dp", scatter_dimension=2, tiled=True),
        lax.psum_scatter(local_grads[2], "dp", scatter_dimension=1, tiled=True),
        lax.psum_scatter(local_grads[3], "dp", scatter_dimension=2, tiled=True),
        lax.psum_scatter(local_grads[4], "dp", scatter_dimension=1, tiled=True),
        lax.psum_scatter(local_grads[5], "dp", scatter_dimension=1, tiled=True),
        lax.psum_scatter(vector_grad, "dp", scatter_dimension=2, tiled=True),
    )
    grad_scale = grad_gain / math.sqrt(tokens.shape[0] * lax.axis_size("dp"))
    old_params = (w_qkv, b_qkv, w_out, w_up, b_up, w_down, vectors)
    states = (
        state_qkv,
        state_qkv_bias,
        state_out,
        state_up,
        state_up_bias,
        state_down,
        state_vectors,
    )
    decays = (weight_decay, 0.0, weight_decay, weight_decay, 0.0, weight_decay, 0.0)
    scaled = []
    updated = []
    fresh = []
    for number in range(7):
        gradient = summed[number] * grad_scale
        change, moments = adam_step(
            old_params[number].astype(jnp.float32), gradient, states[number], decays[number]
        )
        scaled.append(gradient)
        updated.append(change)
        fresh.append(moments)
    return (
        result,
        grad_tokens,
        scaled[0],
        scaled[1],
        scaled[2],
        scaled[3],
        scaled[4],
        scaled[5],
        scaled[6],
        updated[0],
        updated[1],
        updated[2],
        updated[3],
        updated[4],
        updated[5],
        updated[6],
        fresh[0],
        fresh[1],
        fresh[2],
        fresh[3],
        fresh[4],
        fresh[5],
        fresh[6],
    )


def solution(mesh):
    placed = (
        P("dp", ("row", "col")),
        P("dp", ("row", "col")),
        P("row", None, "col", "dp"),
        P(None, "col", "dp"),
        P("col", "dp", "row"),
        P("row", "col", "dp"),
        P("col", "dp"),
        P("col", "dp", "row"),
        P(None, ("row", "col"), "dp"),
        P(None, "row", None, "col", "dp"),
        P(None, None, "col", "dp"),
        P(None, "col", "dp", "row"),
        P(None, "row", "col", "dp"),
        P(None, "col", "dp"),
        P(None, "col", "dp", "row"),
        P(None, None, ("row", "col"), "dp"),
    )
    return jax.shard_map(
        on_device,
        mesh=mesh,
        in_specs=placed,
        out_specs=(
            P("dp", ("row", "col")),
            P("dp", ("row", "col")),
            P("row", None, "col", "dp"),
            P(None, "col", "dp"),
            P("col", "dp", "row"),
            P("row", "col", "dp"),
            P("col", "dp"),
            P("col", "dp", "row"),
            P(None, ("row", "col"), "dp"),
            P("row", None, "col", "dp"),
            P(None, "col", "dp"),
            P("col", "dp", "row"),
            P("row", "col", "dp"),
            P("col", "dp"),
            P("col", "dp", "row"),
            P(None, ("row", "col"), "dp"),
            P(None, "row", None, "col", "dp"),
            P(None, None, "col", "dp"),
            P(None, "col", "dp", "row"),
            P(None, "row", "col", "dp"),
            P(None, "col", "dp"),
            P(None, "col", "dp", "row"),
            P(None, None, ("row", "col"), "dp"),
        ),
        check_vma=False,
    )
```

profile of v0, /device:TPU:0, one launch (start us, length us, event | category | flops | bytes accessed | tf_op | source)
XLA Modules:
  0.0 1573.7 jit_solution(10341584998933640259)
XLA Ops:
  7.2 10.4 all_gather.47
  18.4 5.2 all_gather.45
  26.5 37.6 %all-reduce.3 = (f32[1576]{0:T(1024)S(1)}, f32[1576]{0:T(1024)S(1)}) all-reduce(f32[1576]{0:T(1024)S(1)} %get-tuple-element.103, f32[1576]{0:T(1024)S(1)} %get-tuple-element.102), channel_id=1, replica_groups=mesh['dp'=4,'row'=4,'col'=2] {'row','col'}, use_global_device_ids=true, to_apply=%region_3.0 | all-reduce | flops 3152 | bytes 25216 | tf_op jit(solution)/shard_map/psum | solution.py:28
  64.7 8.6 all_gather.46
  74.1 5.2 fusion.35
  80.1 5.2 all_gather.48
  85.6 156.0 %reduce-scatter.22.cloned.1.call-done = f32[1576,3,128]{2,0,1:T(8,128)} async-done(((f32[1576,3,512]{2,0,1:T(8,128)}), f32[1576,3,128]{2,0,1:T(8,128)}) %reduce-scatter.22.cloned.1.call-update) | async-done | bytes 2420752 | tf_op jit(solution)/shard_map/reduce_scatter | solution.py:60
  244.5 4.4 reshape.224
  267.0 6.0 all_gather.50
  273.0 33.4 %all-gather.7.cloned.1.call-done = bf16[1576,512]{0,1:T(8,128)(2,1)} async-done(((bf16[1576,128]{0,1:T(8,128)(2,1)}), bf16[1576,512]{0,1:T(8,128)(2,1)}) %all-gather.7.cloned.1.call-update) | async-done | bytes 1613840 | tf_op jit(solution)/shard_map/all_gather | solution.py:64
  306.4 3.3 fusion.69
  312.2 12.3 all_gather.56
  324.5 8.2 convolution_bitcast_fusion
  341.0 11.2 reduce-scatter.24.cloned.1.call-done
  355.2 37.1 %all-reduce.2 = (f32[1576]{0:T(1024)}, f32[1576]{0:T(1024)}) all-reduce(f32[1576]{0:T(1024)} %get-tuple-element.101, f32[1576]{0:T(1024)} %get-tuple-element.100), channel_id=1, replica_groups=mesh['dp'=4,'row'=4,'col'=2] {'row','col'}, use_global_device_ids=true, to_apply=%region_11.0 | all-reduce | flops 3152 | bytes 25216 | tf_op jit(solution)/shard_map/psum | solution.py:28
  395.3 8.7 all_gather.51
  404.0 8.0 convolution_bitcast_fusion.1
  412.1 6.5 all_gather.53
  422.7 167.3 %reduce-scatter.30.cloned.1.call-done = f32[1576,1,512]{2,0,1:T(8,128)} async-done(((f32[1576,1,2048]{2,0,1:T(8,128)}), f32[1576,1,512]{2,0,1:T(8,128)}) %reduce-scatter.30.cloned.1.call-update) | async-done | bytes 3227664 | tf_op jit(solution)/shard_map/reduce_scatter | solution.py:78
  590.0 220.6 %reduce-scatter.26.cloned.1.call-done = f32[1576,1,512]{2,0,1:T(8,128)} async-done(((f32[1576,1,2048]{2,0,1:T(8,128)}), f32[1576,1,512]{2,0,1:T(8,128)}) %reduce-scatter.26.cloned.1.call-update) | async-done | bytes 3227664 | tf_op jit(solution)/shard_map/reduce_scatter | solution.py:60
  810.6 9.9 fusion.9
  820.5 9.1 fusion.4
  829.7 110.0 %all-gather.15.cloned.1.call-done = bf16[1576,1,2048]{2,0,1:T(8,128)(2,1)} async-done(((bf16[1576,1,512]{2,0,1:T(8,128)(2,1)}), bf16[1576,1,2048]{2,0,1:T(8,128)(2,1)}) %all-gather.15.cloned.1.call-update) | async-done | bytes 6455312 | tf_op jit(solution)/shard_map/all_gather | solution.py:83
  939.7 6.1 fusion
  946.1 111.5 %all-gather.11.cloned.1.call-done = bf16[1576,2048]{1,0:T(8,128)(2,1)} async-done(((bf16[1576,512]{1,0:T(8,128)(2,1)}), bf16[1576,2048]{1,0:T(8,128)(2,1)}) %all-gather.11.cloned.1.call-update) | async-done | bytes 6455312 | tf_op jit(solution)/shard_map/all_gather | solution.py:64
  1057.6 6.1 fusion.70
  1066.6 18.0 %reduce-scatter.32.cloned.1.call-done = f32[1576,128]{1,0:T(8,128)} async-done(((f32[1576,256]{1,0:T(8,128)}), f32[1576,128]{1,0:T(8,128)}) %reduce-scatter.32.cloned.1.call-update) | async-done | bytes 806928 | tf_op jit(solution)/shard_map/reduce_scatter | solution.py:53
  1087.5 37.2 %all-reduce.1 = (f32[1576]{0:T(1024)}, f32[1576]{0:T(1024)}) all-reduce(f32[1576]{0:T(1024)} %get-tuple-element.93, f32[1576]{0:T(1024)} %get-tuple-element.97), channel_id=1, replica_groups=mesh['dp'=4,'row'=4,'col'=2] {'row','col'}, use_global_device_ids=true, to_apply=%region_19.0 | all-reduce | flops 3152 | bytes 25216 | tf_op jit(solution)/shard_map/psum | solution.py:39
  1126.0 4.0 convert_reduce_fusion.3
  1130.0 8.6 all_gather.58
  1141.9 59.0 %reduce-scatter.34.cloned.1.call-done = f32[1576,1,128]{2,0,1:T(8,128)} async-done(((f32[1576,1,512]{2,0,1:T(8,128)}), f32[1576,1,128]{2,0,1:T(8,128)}) %reduce-scatter.34.cloned.1.call-update) | async-done | bytes 806928 | tf_op jit(solution)/shard_map/reduce_scatter | solution.py:78
  1217.7 9.8 copy.128
  1227.5 4.3 convert_reduce_fusion
  1232.6 6.4 fusion.33
  1239.1 6.6 fusion.73
  1247.4 66.2 %all-gather.17.cloned.1.call-done = bf16[1576,3,512]{0,2,1:T(8,128)(2,1)} async-done(((bf16[1576,3,128]{0,2,1:T(8,128)(2,1)}), bf16[1576,3,512]{0,2,1:T(8,128)(2,1)}) %all-gather.17.cloned.1.call-update) | async-done | bytes 4841488 | tf_op jit(solution)/shard_map/all_gather | solution.py:83
  1313.6 3.2 convert_reduce_fusion.1
  1317.9 5.3 fusion.31
  1324.2 10.2 reduce-scatter.48.cloned.1.call-done
  1335.2 5.3 fusion.71
  1344.8 23.5 %reduce-scatter.42.cloned.1.call-done = f32[256,32,16]{0,2,1:T(8,128)} async-done(((f32[256,32,64]{0,2,1:T(8,128)}), f32[256,32,16]{0,2,1:T(8,128)}) %reduce-scatter.42.cloned.1.call-update) | async-done | bytes 524304 | tf_op jit(solution)/shard_map/reduce_scatter | solution.py:265
  1370.6 31.6 %reduce-scatter.44.cloned.1.call-done = f32[32,16,256]{2,1,0:T(8,128)} async-done(((f32[32,64,256]{2,1,0:T(8,128)}), f32[32,16,256]{2,1,0:T(8,128)}) %reduce-scatter.44.cloned.1.call-update) | async-done | bytes 524304 | tf_op jit(solution)/shard_map/reduce_scatter | solution.py:267
  1407.1 19.2 %reduce-scatter.40.cloned.1.call-done = f32[8,16,256]{2,1,0:T(8,128)} async-done(((f32[8,64,256]{2,1,0:T(8,128)}), f32[8,16,256]{2,1,0:T(8,128)}) %reduce-scatter.40.cloned.1.call-update) | async-done | bytes 131088 | tf_op jit(solution)/shard_map/reduce_scatter | solution.py:264
  1429.8 18.8 %reduce-scatter.46.cloned.1.call-done = f32[16,16]{1,0:T(8,128)} async-done(((f32[64,16]{1,0:T(8,128)}), f32[16,16]{1,0:T(8,128)}) %reduce-scatter.46.cloned.1.call-update) | async-done | bytes 1040
  1450.7 28.6 %reduce-scatter.38.cloned.1.call-done = f32[256,3,8,16]{0,3,2,1:T(8,128)} async-done(((f32[256,3,8,64]{0,3,2,1:T(8,128)}), f32[256,3,8,16]{0,3,2,1:T(8,128)}) %reduce-scatter.38.cloned.1.call-update) | async-done | bytes 393232 | tf_op jit(solution)/shard_map/reduce_scatter | solution.py:262
  1482.7 25.4 %reduce-scatter.36.cloned.1.call-done = f32[1576,128]{1,0:T(8,128)} async-done(((f32[1576,256]{1,0:T(8,128)}), f32[1576,128]{1,0:T(8,128)}) %reduce-scatter.36.cloned.1.call-update) | async-done | bytes 806928 | tf_op jit(solution)/shard_map/reduce_scatter | solution.py:53
  1510.2 36.2 %all-reduce = (f32[1576]{0:T(1024)S(1)}, f32[1576]{0:T(1024)S(1)}) all-reduce(f32[1576]{0:T(1024)S(1)} %get-tuple-element.95, f32[1576]{0:T(1024)S(1)} %get-tuple-element.96), channel_id=1, replica_groups=mesh['dp'=4,'row'=4,'col'=2] {'row','col'}, use_global_device_ids=true, to_apply=%region_26.0 | all-reduce | flops 3152 | bytes 25216 | tf_op jit(solution)/shard_map/psum | solution.py:39
  1550.6 13.7 reduce-scatter.50.cloned.1.call-done
  (273 shorter events, 109.3 us)
Async XLA Ops:
  7.2 57.0 %copy-start = (f32[1576,128]{1,0:T(8,128)S(1)}, f32[1576,128]{1,0:T(8,128)}, u32[]{:S(2)}) copy-start(f32[1576,128]{1,0:T(8,128)} %param.16) | copy-start | bytes 2420740
  7.2 234.4 %reduce-scatter.22.cloned.1.call-start = ((), (), s32[]{:S(2)}) async-start(), calls=%async_computation.15 | async-start | bytes 12103680 | tf_op jit(solution)/shard_map/reduce_scatter | solution.py:60
  17.6 61.7 %copy-start.17 = (bf16[256,3,8,64]{0,3,2,1:T(8,128)(2,1)}, bf16[256,3,8,64]{0,3,2,1:T(8,128)(2,1)S(1)}, u32[]{:S(2)}) copy-start(bf16[256,3,8,64]{0,3,2,1:T(8,128)(2,1)S(1)} %all_gather.47) | copy-start | bytes 2359300
  24.9 54.4 %copy-start.46 = (f32[128]{0:T(128)}, f32[128]{0:T(128)S(1)}, u32[]{:S(2)}) copy-start(f32[128]{0:T(128)S(1)} %mul.531) | copy-start | bytes 1540
  79.3 227.0 %all-gather.7.cloned.1.call-start = ((), (), s32[]{:S(2)}) async-start(), calls=%async_computation.16 | async-start | bytes 2129920 | tf_op jit(solution)/shard_map/all_gather | solution.py:64
  266.2 58.3 %all-gather.13.cloned.1.call-start = ((), (), s32[]{:S(2)}) async-start(), calls=%async_computation.21 | async-start | bytes 1310720 | tf_op jit(solution)/shard_map/all_gather | solution.py:184
  266.9 85.3 %reduce-scatter.24.cloned.1.call-start = ((), (), s32[]{:S(2)}) async-start(), calls=%async_computation.17 | async-start | bytes 2420736 | tf_op jit(solution)/shard_map/reduce_scatter | solution.py:53
  309.7 94.4 %all-gather.9.cloned.1.call-start = ((), (), s32[]{:S(2)}) async-start(), calls=%async_computation.18 | async-start | bytes 1310720 | tf_op jit(solution)/shard_map/all_gather | solution.py:182
  310.2 279.8 %reduce-scatter.30.cloned.1.call-start = ((), (), s32[]{:S(2)}) async-start(), calls=%async_computation.23 | async-start | bytes 16138240 | tf_op jit(solution)/shard_map/reduce_scatter | solution.py:78
  332.7 477.9 %reduce-scatter.26.cloned.1.call-start = ((), (), s32[]{:S(2)}) async-start(), calls=%async_computation.19 | async-start | bytes 16138240 | tf_op jit(solution)/shard_map/reduce_scatter | solution.py:60
  412.0 527.7 %all-gather.15.cloned.1.call-start = ((), (), s32[]{:S(2)}) async-start(), calls=%async_computation.24 | async-start | bytes 8069120 | tf_op jit(solution)/shard_map/all_gather | solution.py:83
  820.5 237.1 %all-gather.11.cloned.1.call-start = ((), (), s32[]{:S(2)}) async-start(), calls=%async_computation.20 | async-start | bytes 8069120 | tf_op jit(solution)/shard_map/all_gather | solution.py:64
  829.6 254.9 %reduce-scatter.32.cloned.1.call-start = ((), (), s32[]{:S(2)}) async-start(), calls=%async_computation.25 | async-start | bytes 2420736 | tf_op jit(solution)/shard_map/reduce_scatter | solution.py:53
  945.9 180.2 %reduce-scatter.28.cloned.1.call-start = ((), (), s32[]{:S(2)}) async-start(), calls=%async_computation.22 | async-start | bytes 2420736 | tf_op jit(solution)/shard_map/reduce_scatter | solution.py:53
  1063.7 137.2 %reduce-scatter.34.cloned.1.call-start = ((), (), s32[]{:S(2)}) async-start(), calls=%async_computation.26 | async-start | bytes 4034560 | tf_op jit(solution)/shard_map/reduce_scatter | solution.py:78
  1141.8 171.8 %all-gather.17.cloned.1.call-start = ((), (), s32[]{:S(2)}) async-start(), calls=%async_computation.27 | async-start | bytes 6389760 | tf_op jit(solution)/shard_map/all_gather | solution.py:83
  1217.4 116.9 %reduce-scatter.48.cloned.1.call-start = ((), (), s32[]{:S(2)}) async-start(), calls=%async_computation.34 | async-start | bytes 40960
  1232.6 135.7 %reduce-scatter.42.cloned.1.call-start = ((), (), s32[]{:S(2)}) async-start(), calls=%async_computation.31 | async-start | bytes 2621440 | tf_op jit(solution)/shard_map/reduce_scatter | solution.py:265
  1239.1 163.1 %reduce-scatter.44.cloned.1.call-start = ((), (), s32[]{:S(2)}) async-start(), calls=%async_computation.32 | async-start | bytes 2621440 | tf_op jit(solution)/shard_map/reduce_scatter | solution.py:267
  1245.8 180.5 %reduce-scatter.40.cloned.1.call-start = ((), (), s32[]{:S(2)}) async-start(), calls=%async_computation.30 | async-start | bytes 655360 | tf_op jit(solution)/shard_map/reduce_scatter | solution.py:264
  1247.3 70.5 %copy-start.13 = (bf16[1576,256]{1,0:T(8,128)(2,1)S(1)}, bf16[1576,256]{1,0:T(8,128)(2,1)}, u32[]{:S(2)}) copy-start(bf16[1576,256]{1,0:T(8,128)(2,1)} %copy-done.12) | copy-start | bytes 2420740
  1247.3 201.3 %reduce-scatter.46.cloned.1.call-start = ((), (), s32[]{:S(2)}) async-start(), calls=%async_computation.33 | async-start | bytes 40960
  1317.8 161.6 %reduce-scatter.38.cloned.1.call-start = ((), (), s32[]{:S(2)}) async-start(), calls=%async_computation.29 | async-start | bytes 1966080 | tf_op jit(solution)/shard_map/reduce_scatter | solution.py:262
  1323.2 184.9 %reduce-scatter.36.cloned.1.call-start = ((), (), s32[]{:S(2)}) async-start(), calls=%async_computation.28 | async-start | bytes 2420736 | tf_op jit(solution)/shard_map/reduce_scatter | solution.py:53
  1335.2 33.0 %copy-start.8 = (f32[2,256,32,16]{1,3,2,0:T(8,128)S(1)}, f32[2,256,32,16]{1,3,2,0:T(8,128)}, u32[]{:S(2)}) copy-start(f32[2,256,32,16]{1,3,2,0:T(8,128)} %param.28) | copy-start | bytes 3145732
  1340.5 61.7 %copy-start.9 = (f32[2,32,16,256]{3,2,1,0:T(8,128)S(1)}, f32[2,32,16,256]{3,2,1,0:T(8,128)}, u32[]{:S(2)}) copy-start(f32[2,32,16,256]{3,2,1,0:T(8,128)} %param.30) | copy-start | bytes 3145732
  1340.5 223.8 %reduce-scatter.50.cloned.1.call-start = ((), (), s32[]{:S(2)}) async-start(), calls=%async_computation.35 | async-start | bytes 40960
  1369.5 35.1 %copy-start.20 = (f32[256,32,16]{0,2,1:T(8,128)}, f32[256,32,16]{0,2,1:T(8,128)S(1)}, u32[]{:S(2)}) copy-start(f32[256,32,16]{0,2,1:T(8,128)S(1)} %get-tuple-element.115) | copy-start | bytes 1572868
  1369.5 35.1 %copy-start.22 = (f32[256,32,16]{0,2,1:T(8,128)S(1)}, f32[256,32,16]{0,2,1:T(8,128)}, u32[]{:S(2)}) copy-start(f32[256,32,16]{0,2,1:T(8,128)} %reduce-scatter.42.cloned.1.call-done) | copy-start | bytes 1572868
  1369.5 35.1 %copy-start.27 = (bf16[256,32,16]{0,2,1:T(8,128)(2,1)S(1)}, bf16[256,32,16]{0,2,1:T(8,128)(2,1)}, u32[]{:S(2)}) copy-start(bf16[256,32,16]{0,2,1:T(8,128)(2,1)} %param.21) | copy-start | bytes 786436
  1404.6 23.5 %copy-start.31 = (bf16[8,16,256]{2,1,0:T(8,128)(2,1)S(1)}, bf16[8,16,256]{2,1,0:T(8,128)(2,1)}, u32[]{:S(2)}) copy-start(bf16[8,16,256]{2,1,0:T(8,128)(2,1)} %param.20) | copy-start | bytes 196612
  1404.6 44.9 %copy-start.38 = (f32[2,2,8,16]{3,2,1,0:T(8,128)S(1)}, f32[2,2,8,16]{3,2,1,0:T(8,128)}, u32[]{:S(2)}) copy-start(f32[2,2,8,16]{3,2,1,0:T(8,128)} %param.26) | copy-start | bytes 6148
  1405.8 44.3 %copy-start.43 = (bf16[2,8,16]{2,1,0:T(8,128)(2,1)S(1)}, bf16[2,8,16]{2,1,0:T(8,128)(2,1)}, u32[]{:S(2)}) copy-start(bf16[2,8,16]{2,1,0:T(8,128)(2,1)} %param.19) | copy-start | bytes 1540
  1405.8 73.5 %copy-start.19 = (f32[2,256,3,8,16]{1,4,3,2,0:T(8,128)S(1)}, f32[2,256,3,8,16]{1,4,3,2,0:T(8,128)}, u32[]{:S(2)}) copy-start(f32[2,256,3,8,16]{1,4,3,2,0:T(8,128)} %param.25) | copy-start | bytes 2359300
  1407.1 74.6 %copy-start.29 = (bf16[256,3,8,16]{0,3,2,1:T(8,128)(2,1)S(1)}, bf16[256,3,8,16]{0,3,2,1:T(8,128)(2,1)}, u32[]{:S(2)}) copy-start(bf16[256,3,8,16]{0,3,2,1:T(8,128)(2,1)} %param.18) | copy-start | bytes 589828
  1429.8 78.3 %copy-start.1 = (f32[1576,128]{1,0:T(8,128)S(1)}, f32[1576,128]{1,0:T(8,128)}, u32[]{:S(2)}) copy-start(f32[1576,128]{1,0:T(8,128)} %param.16) | copy-start | bytes 2420740
  1429.8 78.3 %copy-start.33 = (f32[1576]{0:T(1024)S(1)}, f32[1576]{0:T(1024)}, u32[]{:S(2)}) copy-start(f32[1576]{0:T(1024)} %copy-done.32) | copy-start | bytes 18916
  1429.8 78.3 %copy-start.35 = (f32[1576]{0:T(1024)S(1)}, f32[1576]{0:T(1024)}, u32[]{:S(2)}) copy-start(f32[1576]{0:T(1024)} %copy-done.34) | copy-start | bytes 18916
  1429.8 78.3 %copy-start.47 = (f32[128]{0:T(128)S(1)}, f32[128]{0:T(128)}, u32[]{:S(2)}) copy-start(f32[128]{0:T(128)} %copy-done.46) | copy-start | bytes 1540
  1449.5 60.8 %copy-start.39 = (f32[2,8,16]{2,1,0:T(8,128)}, f32[2,8,16]{2,1,0:T(8,128)S(1)}, u32[]{:S(2)}) copy-start(f32[2,8,16]{2,1,0:T(8,128)S(1)} %get-tuple-element.119) | copy-start | bytes 3076
  1480.6 70.0 %copy-start.25 = (f32[256,3,8,16]{0,3,2,1:T(8,128)}, f32[256,3,8,16]{0,3,2,1:T(8,128)S(1)}, u32[]{:S(2)}) copy-start(f32[256,3,8,16]{0,3,2,1:T(8,128)S(1)} %get-tuple-element.121) | copy-start | bytes 1179652
  1480.6 66.0 %copy-start.51 = (f32[1,2,64]{2,1,0:T(2,128)S(1)}, f32[1,2,64]{2,1,0:T(2,128)}, u32[]{:S(2)}) copy-start(f32[1,2,64]{2,1,0:T(2,128)} %stack.110) | copy-start | bytes 1540
  1480.6 66.0 %copy-start.49 = (f32[1,2,64]{2,1,0:T(2,128)S(1)}, f32[1,2,64]{2,1,0:T(2,128)}, u32[]{:S(2)}) copy-start(f32[1,2,64]{2,1,0:T(2,128)} %stack.111) | copy-start | bytes 1540
  1480.6 66.0 %copy-start.50 = (f32[1,2,64]{2,1,0:T(2,128)S(1)}, f32[1,2,64]{2,1,0:T(2,128)}, u32[]{:S(2)}) copy-start(f32[1,2,64]{2,1,0:T(2,128)} %stack.112) | copy-start | bytes 1540
  1480.6 66.0 %copy-start.48 = (f32[1,2,64]{2,1,0:T(2,128)S(1)}, f32[1,2,64]{2,1,0:T(2,128)}, u32[]{:S(2)}) copy-start(f32[1,2,64]{2,1,0:T(2,128)} %stack.113) | copy-start | bytes 1540
  1480.6 66.9 %copy-start.16 = (f32[1576,128]{1,0:T(8,128)S(1)}, f32[1576,128]{1,0:T(8,128)}, u32[]{:S(2)}) copy-start(f32[1576,128]{1,0:T(8,128)} %get-tuple-element.129) | copy-start | bytes 2420740
  1482.7 82.5 %copy-start.44 = (bf16[6,2,16]{2,1,0:T(2,128)(2,1)S(1)}, bf16[6,2,16]{2,1,0:T(2,128)(2,1)}, u32[]{:S(2)}) copy-start(bf16[6,2,16]{2,1,0:T(2,128)(2,1)} %param.24) | copy-start | bytes 1156
  1482.7 82.5 %copy-start.45 = (f32[2,6,2,16]{3,2,1,0:T(2,128)S(1)}, f32[2,6,2,16]{3,2,1,0:T(2,128)}, u32[]{:S(2)}) copy-start(f32[2,6,2,16]{3,2,1,0:T(2,128)} %param.31) | copy-start | bytes 4612
  (29 other events, 171.5 us)
Sparse Core Ops, SparseCore 0:
  79.5 162.1 reduce-scatter.21
  266.3 40.0 all-gather.6
  307.9 15.5 all-gather.12
  325.6 26.5 reduce-scatter.23
  353.7 16.7 all-gather.8
  372.8 217.1 reduce-scatter.29
  592.4 218.1 reduce-scatter.25
  820.6 119.0 all-gather.14
  941.4 116.2 all-gather.10
  1059.8 24.6 reduce-scatter.31
  1086.8 27.3 reduce-scatter.27
  1141.9 58.9 reduce-scatter.33
  1217.6 95.9 all-gather.16
  1316.5 17.7 reduce-scatter.47
  1336.7 31.4 reduce-scatter.41
  1370.8 31.4 reduce-scatter.43
  1404.6 21.6 reduce-scatter.39
  1429.2 19.3 reduce-scatter.45
  1451.1 28.1 reduce-scatter.37
  1481.6 26.5 reduce-scatter.35
  1547.7 16.5 reduce-scatter.49
where the time goes:
time: 1580 us; the launch traced here: 1570 us
  waiting for transfers between devices  1130 us (72%)
  blocking collectives  220 us (14%)
  other arithmetic  74.6 us (5%)
  matrix products  70.8 us (4%)
  local copies, waits for them, and re-layouts  65.9 us (4%)
    reduce_scatter x2, waiting for transfers between devices, project_in(): lax.psum_scatter(partial_value, 'row', scatter_dimension=2, tiled=True)  377 us
    reduce_scatter x2, waiting for transfers between devices, back_out(): lax.psum_scatter(partial_value, 'row', scatter_dimension=2, tiled=True)  226 us
    all_gather x2, waiting for transfers between devices, back_in(): grad_cols = lax.all_gather(grad_low, 'row', axis=2, tiled=True)  176 us
    all_gather x2, waiting for transfers between devices, project_out(): gathered = lax.all_gather(mixed, 'row', axis=1, tiled=True)  145 us
    psum x2, blocking collectives, norm_forward(): lax.psum((jnp.sum(stream, axis=1), jnp.sum(stream * stream, axis=1)), ('r...  74.7 us
    psum x2, blocking collectives, norm_backward(): lax.psum((jnp.sum(weighted, axis=1), jnp.sum(weighted * scaled, axis=1)),...  73.4 us
    reduce_scatter x4, waiting for transfers between devices, col_total(): lax.psum_scatter(partial_value, 'col', scatter_dimension=1, tiled=True)  54.7 us
    unnamed x24, waiting for transfers between devices  44.2 us
  transfers between devices with their start and end apart: 21, of which 18 were waited for; matrix products, arithmetic and copies ran while one was open for 9% of the time, Pallas kernels for 0%

commit v1 on v0

v1 whole, which is shorter than its diff:
```python
import math

import jax
import jax.numpy as jnp
from jax import lax
from jax.sharding import PartitionSpec as P

HD = 64
SEQ = 197
STEP = 10

norm_eps = 1e-06
beta_first = 0.9
beta_second = 0.999
learn_rate = 0.01
weight_decay = 0.05
adam_eps = 1e-08
grad_gain = 32.0

LOW = jnp.bfloat16
WIDE = jnp.float32


def turn(values, shift):
    count = lax.axis_size("row")
    return lax.ppermute(values, "row", [(i, (i + shift) % count) for i in range(count)])


def swap_col(values):
    return lax.ppermute(values, "col", [(0, 1), (1, 0)])


def swap_dp(values, bit):
    count = lax.axis_size("dp")
    return lax.ppermute(values, "dp", [(i, i ^ bit) for i in range(count)])


def dp_bits():
    bits = []
    bit = 1
    while bit < lax.axis_size("dp"):
        bits.append(bit)
        bit *= 2
    return bits


def gather_row(values):
    return [values] + [turn(values, k) for k in range(1, lax.axis_size("row"))]


def gather_dp(values):
    blocks = {0: values}
    for bit in reversed(dp_bits()):
        for place in list(blocks):
            blocks[place ^ bit] = swap_dp(blocks[place], bit)
    return [blocks[d] for d in range(len(blocks))]


def scatter_dp(blocks, kind):
    held = dict(enumerate(blocks))
    for bit in dp_bits():
        for place in [d for d in held if not d & bit]:
            came = swap_dp(held.pop(place ^ bit), bit)
            held[place] = (held[place].astype(WIDE) + came.astype(WIDE)).astype(kind)
    return held[0]


def scatter_row(blocks):
    total = blocks[0].astype(WIDE)
    for k in range(1, len(blocks)):
        total = total + turn(blocks[k], -k).astype(WIDE)
    return total


def xor_order(values, axis):
    mine = lax.axis_index("dp")
    shape = values.shape
    for bit in dp_bits():
        split = values.reshape(shape[:axis] + (shape[axis] // (2 * bit), 2, bit) + shape[axis + 1 :])
        flipped = jnp.flip(split, axis + 1)
        values = jnp.where((mine & bit) > 0, flipped, split).reshape(shape)
    return values


def exact_gelu(values):
    return jax.nn.gelu(values, approximate=False)


def adam_step(weight_old, gradient, moments, decay_on):
    first_moment = beta_first * moments[0] + (1.0 - beta_first) * gradient
    second_moment = beta_second * moments[1] + (1.0 - beta_second) * gradient * gradient
    first_hat = first_moment / (1.0 - beta_first**STEP)
    second_hat = second_moment / (1.0 - beta_second**STEP)
    change = -learn_rate * (first_hat / (jnp.sqrt(second_hat) + adam_eps) + decay_on * weight_old)
    return (change, jnp.stack([first_moment, second_moment]))


def dot_nt(left, right):
    return jnp.einsum("nta,fa->ntf", left, right, preferred_element_type=WIDE)


def dot_nn(left, right):
    return jnp.einsum("ntf,fa->nta", left, right, preferred_element_type=WIDE)


def dot_tn(left, right):
    return jnp.einsum("ntf,nta->fa", left, right, preferred_element_type=WIDE)


def norm_forward(stream, gain, shift):
    center = jnp.mean(stream, axis=-1, keepdims=True)
    offset = stream - center
    inv_std = lax.rsqrt(jnp.mean(offset * offset, axis=-1, keepdims=True) + norm_eps)
    scaled = offset * inv_std
    return (scaled * gain + shift).astype(LOW), scaled, inv_std


def norm_backward(grad_norm, scaled, inv_std, gain):
    weighted = grad_norm * gain
    return inv_std * (
        weighted
        - jnp.mean(weighted, axis=-1, keepdims=True)
        - scaled * jnp.mean(weighted * scaled, axis=-1, keepdims=True)
    )


def attend(packed_low, heads):
    split = packed_low.reshape(packed_low.shape[0], SEQ, 3, heads, HD)
    scores = jnp.einsum("nqhe,nkhe->nhqk", split[:, :, 0], split[:, :, 1], preferred_element_type=WIDE) * (1.0 / math.sqrt(HD))
    row_max = jnp.max(scores, axis=-1, keepdims=True)
    log_total = row_max + jnp.log(jnp.sum(jnp.exp(scores - row_max), axis=-1, keepdims=True))
    weights = jnp.exp(scores - log_total).astype(LOW)
    attended = jnp.einsum("nhqk,nkhe->nqhe", weights, split[:, :, 2], preferred_element_type=WIDE)
    return attended.reshape(packed_low.shape[0], SEQ, -1).astype(LOW), log_total


def attend_back(packed_low, log_total, grad_low, heads):
    split = packed_low.reshape(packed_low.shape[0], SEQ, 3, heads, HD)
    queries, key_rows, values = split[:, :, 0], split[:, :, 1], split[:, :, 2]
    score_scale = 1.0 / math.sqrt(HD)
    scores = jnp.einsum("nqhe,nkhe->nhqk", queries, key_rows, preferred_element_type=WIDE) * score_scale
    weights = jnp.exp(scores - log_total)
    grad_heads = grad_low.reshape(queries.shape)
    grad_values = jnp.einsum("nhqk,nqhe->nkhe", weights.astype(LOW), grad_heads, preferred_element_type=WIDE)
    grad_weights = jnp.einsum("nqhe,nkhe->nhqk", grad_heads, values, preferred_element_type=WIDE)
    grad_scores = weights * (grad_weights - jnp.sum(grad_weights * weights, axis=-1, keepdims=True))
    grad_scores = grad_scores.astype(LOW)
    grad_queries = jnp.einsum("nhqk,nkhe->nqhe", grad_scores, key_rows, preferred_element_type=WIDE) * score_scale
    grad_keys = jnp.einsum("nhqk,nqhe->nkhe", grad_scores, queries, preferred_element_type=WIDE) * score_scale
    stacked = jnp.stack([grad_queries, grad_keys, grad_values], axis=2)
    return stacked.reshape(packed_low.shape[0], SEQ, -1).astype(LOW)


def on_device(
    tokens, cotangent, w_qkv, b_qkv, w_out, w_up, b_up, w_down, vectors,
    state_qkv, state_qkv_bias, state_out, state_up, state_up_bias, state_down, state_vectors,
):
    parts, rows = lax.axis_size("dp"), lax.axis_size("row")
    low_col = lax.axis_index("col") == 0
    row_index = lax.axis_index("row")
    width = w_qkv.shape[0]
    heads, chunk = w_qkv.shape[2], w_qkv.shape[3]
    groups = w_up.shape[1]
    strip = tokens.shape[1]
    images = tokens.shape[0] // (SEQ * rows)

    qkv_own = w_qkv.transpose(1, 2, 3, 0).reshape(-1, width)
    out_own = w_out.reshape(-1, width)
    up_own = w_up.transpose(1, 2, 0).reshape(-1, width)
    down_own = w_down.reshape(-1, width)

    vec_own = vectors.reshape(-1)
    vec_far = swap_col(vec_own)
    vec_pair = jnp.stack([jnp.where(low_col, vec_own, vec_far), jnp.where(low_col, vec_far, vec_own)])

    def to_images(stream):
        blocks = stream.astype(LOW).reshape(rows, images, SEQ, strip)
        came = [lax.dynamic_index_in_dim(blocks, row_index, 0, False)]
        for k in range(1, rows):
            came.append(turn(lax.dynamic_index_in_dim(blocks, (row_index + k) % rows, 0, False), k))
        near = jnp.stack(came)
        far = swap_col(near)
        both = jnp.stack([jnp.where(low_col, near, far), jnp.where(low_col, far, near)])
        return both.transpose(2, 3, 1, 0, 4).reshape(images, SEQ, -1)

    def own_strips(stream):
        split = stream.reshape(images, SEQ, rows, 2, strip)
        return (
            jnp.where(low_col, split[:, :, :, 0], split[:, :, :, 1]),
            jnp.where(low_col, split[:, :, :, 1], split[:, :, :, 0]),
        )

    def from_images(strips):
        came = [strips[:, :, 0]] + [turn(strips[:, :, k], -k) for k in range(1, rows)]
        stacked = jnp.stack(came)
        order = (jnp.arange(rows) - row_index) % rows
        return stacked[order].reshape(-1, strip).astype(WIDE)

    stream = to_images(tokens).astype(WIDE)

    small_own = jnp.concatenate([b_qkv.reshape(-1), b_up.reshape(-1)])
    vec_blocks = gather_row(vec_pair.reshape(-1))
    small_rows = jnp.stack([jnp.concatenate([small_own, block]) for block in vec_blocks])
    small_size = small_rows.shape[1]
    pad = -small_size % (16 * width)
    small_rows = jnp.pad(small_rows, ((0, 0), (0, pad))).reshape(rows, -1, width)
    first = jnp.concatenate([jnp.stack(gather_row(qkv_own)), small_rows], axis=1)
    first_all = jnp.stack(gather_dp(first))
    second_all = jnp.stack(gather_dp(jnp.stack(gather_row(jnp.concatenate([out_own, up_own])))))
    third_all = jnp.stack(gather_dp(jnp.stack(gather_row(down_own))))

    qkv_count = qkv_own.shape[0]
    small = first_all[:, :, qkv_count:].reshape(parts, rows, -1)[:, :, :small_size]
    bias_qkv = small[:, 0, : 2 * heads * chunk].reshape(parts, 2, heads, chunk).transpose(1, 2, 0, 3).reshape(2, -1).astype(WIDE)
    at = 2 * heads * chunk
    bias_up = small[:, 0, at : at + groups * chunk].reshape(-1).astype(WIDE)
    at = at + groups * chunk
    vec = xor_order(small[:, :, at:].reshape(parts, rows, 2, 6, 2, chunk), 0)
    vec = vec.transpose(3, 1, 2, 4, 0, 5).reshape(6, -1).astype(WIDE)

    def flat(blocks):
        return blocks.transpose(0, 2, 1, 3).reshape(-1, rows * width)

    qkv_flat = flat(
        first_all[:, :, :qkv_count].reshape(parts, rows, 3 * heads, chunk, width).transpose(2, 1, 0, 3, 4).reshape(3 * heads, rows, -1, width)
    )
    out_count = out_own.shape[0]
    out_flat = flat(second_all[:, :, :out_count].reshape(parts, rows, heads, chunk, width).transpose(2, 1, 0, 3, 4).reshape(heads, rows, -1, width))
    up_flat = flat(second_all[:, :, out_count:])
    down_flat = flat(third_all)

    grad_stream = to_images(cotangent)
    grad_wide = grad_stream.astype(WIDE)

    normed_one, scaled_one, inv_one = norm_forward(stream, vec[0], vec[1])
    packed = dot_nt(normed_one, qkv_flat)
    packed = packed + jnp.concatenate([bias_qkv[0], jnp.zeros_like(bias_qkv[0]), bias_qkv[1]])
    packed_low = packed.astype(LOW)
    heads_low, log_total = attend(packed_low, heads)
    branch = dot_nn(heads_low, out_flat).astype(LOW)
    middle = stream + (branch.astype(WIDE) + swap_col(branch).astype(WIDE) + vec[2])
    normed_two, scaled_two, inv_two = norm_forward(middle, vec[3], vec[4])
    hidden = dot_nt(normed_two, up_flat) + bias_up
    activated, gelu_pull = jax.vjp(exact_gelu, hidden)
    units_low = activated.astype(LOW)
    mixed = dot_nn(units_low, down_flat)
    mixed_near, mixed_far = own_strips(mixed)
    top = own_strips(middle + vec[5])[0] + mixed_near + swap_col(mixed_far.astype(LOW)).astype(WIDE)
    result = from_images(top.astype(LOW))

    grad_hidden = gelu_pull(dot_nt(grad_stream, down_flat))[0].astype(LOW)
    up_back = dot_nn(grad_hidden, up_flat).astype(LOW)
    grad_normed_two = up_back.astype(WIDE) + swap_col(up_back).astype(WIDE)
    down_grad = dot_tn(units_low, grad_stream)
    up_grad = dot_tn(grad_hidden, normed_two)
    grad_middle = grad_wide + norm_backward(grad_normed_two, scaled_two, inv_two, vec[3])
    grad_branch = grad_middle.astype(LOW)
    grad_heads = dot_nt(grad_branch, out_flat).astype(LOW)
    out_grad = dot_tn(heads_low, grad_branch)
    grad_packed = attend_back(packed_low, log_total, grad_heads, heads)
    qkv_grad = dot_tn(grad_packed, normed_one)
    back_one = dot_nn(grad_packed, qkv_flat).astype(LOW)
    grad_normed_one = back_one.astype(WIDE) + swap_col(back_one).astype(WIDE)
    grad_tokens = grad_middle + norm_backward(grad_normed_one, scaled_one, inv_one, vec[0])
    grad_tokens = from_images(own_strips(grad_tokens)[0].astype(LOW))

    def to_blocks(grad, lead):
        split = grad.astype(LOW).reshape(lead, parts, chunk, rows, width)
        return split.transpose(1, 3, 0, 2, 4).reshape(parts, rows, -1, width)

    def to_unit_blocks(grad):
        return grad.astype(LOW).reshape(parts, -1, rows, width).transpose(0, 2, 1, 3)

    feed = jnp.concatenate([to_unit_blocks(up_grad), to_unit_blocks(down_grad)], axis=2)
    feed = scatter_dp([feed[d] for d in range(parts)], LOW)
    feed = scatter_row([feed[k] for k in range(rows)])
    attn = jnp.concatenate([to_blocks(qkv_grad, 3 * heads), to_blocks(out_grad, heads)], axis=2)
    attn = scatter_dp([attn[d] for d in range(parts)], LOW)
    attn = scatter_row([attn[k] for k in range(rows)])

    token_sum = lambda v: jnp.sum(v.astype(WIDE), axis=(0, 1))
    vector_sum = jnp.stack([
        token_sum(grad_normed_one * scaled_one),
        token_sum(grad_normed_one),
        token_sum(grad_branch),
        token_sum(grad_normed_two * scaled_two),
        token_sum(grad_normed_two),
        token_sum(grad_stream),
    ])
    packed_sum = token_sum(grad_packed).reshape(3, heads, parts, chunk)
    packed_sum = packed_sum[jnp.array([0, 2])].transpose(2, 0, 1, 3).reshape(parts, -1)
    unit_sum = token_sum(grad_hidden).reshape(parts, -1)
    vector_split = vector_sum.reshape(6, rows, 2, 2, parts, chunk)
    vector_split = jnp.where(low_col, vector_split[:, :, 0], vector_split[:, :, 1])
    vector_split = xor_order(vector_split.transpose(3, 1, 0, 2, 4), 0)
    vector_split = vector_split[:, (row_index - jnp.arange(rows)) % rows]
    tiny = jnp.concatenate([packed_sum, unit_sum, vector_split.reshape(parts, -1)], axis=1)
    tiny = scatter_dp([tiny[d] for d in range(parts)], WIDE)
    tiny = lax.psum(tiny, "row")
    size_packed, size_unit = packed_sum.shape[1], unit_sum.shape[1]
    tiny_vec = tiny[size_packed + size_unit :].reshape(rows, 6, 2, chunk)
    tiny_vec = lax.dynamic_index_in_dim(tiny_vec, row_index, 0, False)

    feed_up, feed_down = feed[: up_own.shape[0]], feed[up_own.shape[0] :]
    attn_qkv, attn_out = attn[:qkv_count], attn[qkv_count:]
    summed = (
        attn_qkv.reshape(3, heads, chunk, width).transpose(3, 0, 1, 2),
        tiny[:size_packed].reshape(b_qkv.shape),
        attn_out.reshape(w_out.shape),
        feed_up.reshape(groups, chunk, width).transpose(2, 0, 1),
        tiny[size_packed : size_packed + size_unit].reshape(b_up.shape),
        feed_down.reshape(w_down.shape),
        tiny_vec,
    )
    grad_scale = grad_gain / math.sqrt(tokens.shape[0] * parts)
    old_params = (w_qkv, b_qkv, w_out, w_up, b_up, w_down, vectors)
    states = (state_qkv, state_qkv_bias, state_out, state_up, state_up_bias, state_down, state_vectors)
    decays = (weight_decay, 0.0, weight_decay, weight_decay, 0.0, weight_decay, 0.0)
    scaled, updated, fresh = [], [], []
    for number in range(7):
        gradient = summed[number] * grad_scale
        change, moments = adam_step(old_params[number].astype(WIDE), gradient, states[number], decays[number])
        scaled.append(gradient)
        updated.append(change)
        fresh.append(moments)
    return (result, grad_tokens, *scaled, *updated, *fresh)


def solution(mesh):
    placed = (
        P("dp", ("row", "col")),
        P("dp", ("row", "col")),
        P("row", None, "col", "dp"),
        P(None, "col", "dp"),
        P("col", "dp", "row"),
        P("row", "col", "dp"),
        P("col", "dp"),
        P("col", "dp", "row"),
        P(None, ("row", "col"), "dp"),
        P(None, "row", None, "col", "dp"),
        P(None, None, "col", "dp"),
        P(None, "col", "dp", "row"),
        P(None, "row", "col", "dp"),
        P(None, "col", "dp"),
        P(None, "col", "dp", "row"),
        P(None, None, ("row", "col"), "dp"),
    )
    params = placed[2:9]
    return jax.shard_map(
        on_device,
        mesh=mesh,
        in_specs=placed,
        out_specs=(placed[0], placed[0], *params, *params, *placed[9:]),
        check_vma=False,
    )
```

time: 1580 us -> 578 us (0.37)
  waiting for transfers between devices: 1130 us -> 189 us
  blocking collectives: 220 us -> 10.8 us
  local copies, waits for them, and re-layouts: 65.9 us -> 177 us
  starting transfers between devices: 1.5 us -> 59.6 us
  matrix products: 70.8 us -> 42.1 us
    reduce_scatter x12 -> x0, waiting for transfers between devices: 761 us -> none  [the longest x2 377 us: project_in(): lax.psum_scatter(partial_value, 'row', scatter_dimension=2, tiled=True)]
    all_gather x6 -> x0, waiting for transfers between devices: 321 us -> none  [the longest x2 176 us: back_in(): grad_cols = lax.all_gather(grad_low, 'row', axis=2, tiled=True)]
    ppermute x0 -> x55, waiting for transfers between devices: none -> 189 us  [the longest x30 105 us: turn(): lax.ppermute(values, 'row', [(i, (i + shift) % count) for i in range(coun...]
    psum x4 -> x1, blocking collectives: 148 us -> 10.8 us  [on_device(): tiny = lax.psum(tiny, 'row')]
    all_gather x9 -> x0, blocking collectives: 71.4 us -> none  [the longest x4 38.2 us: col_pieces(): return lax.all_gather(values, 'col', axis=1, tiled=True)]
    reshape x5 -> x28, local copies, waits for them, and re-layouts: 5.96 us -> 67.6 us  [the longest x4 22.8 us: flat(): return blocks.transpose(0, 2, 1, 3).reshape(-1, rows * width)]
    ppermute x0 -> x55, starting transfers between devices: none -> 59.6 us  [the longest x30 42.6 us: turn(): lax.ppermute(values, 'row', [(i, (i + shift) % count) for i in range(coun...]
    unnamed x24 -> x0, waiting for transfers between devices: 44.2 us -> none
  transfers between devices with their start and end apart: 21 -> 55, of which waited for: 18 -> 18; matrix products, arithmetic and copies ran while one was open for 9% -> 45% of each run, Pallas kernels for 0% -> 0%
where the time goes in v1:
time: 578 us; the launch traced here: 568 us
  waiting for transfers between devices  189 us (33%)
  local copies, waits for them, and re-layouts  177 us (31%)
  other arithmetic  87.9 us (15%)
  starting transfers between devices  59.6 us (10%)
  matrix products  42.1 us (7%)
  blocking collectives  10.8 us (2%)
    ppermute x30, waiting for transfers between devices, turn(): lax.ppermute(values, 'row', [(i, (i + shift) % count) for i in range(coun...  105 us
    ppermute x18, waiting for transfers between devices, swap_dp(): return lax.ppermute(values, 'dp', [(i, i ^ bit) for i in range(count)])  83.1 us
    ppermute x30, starting transfers between devices, turn(): lax.ppermute(values, 'row', [(i, (i + shift) % count) for i in range(coun...  42.6 us
    reshape x4, local copies, waits for them, and re-layouts, flat(): return blocks.transpose(0, 2, 1, 3).reshape(-1, rows * width)  22.8 us
    unnamed x222, local copies, waits for them, and re-layouts  22.6 us
    reshape x2, local copies, waits for them, and re-layouts, to_unit_blocks(): grad.astype(LOW).reshape(parts, -1, rows, width).transpose(0, 2, 1, 3)  15.8 us
    dot_general x4, matrix products, dot_tn(): return jnp.einsum('ntf,nta->fa', left, right, preferred_element_type=WIDE)  14.8 us
    dot_general x4, matrix products, dot_nt(): return jnp.einsum('nta,fa->ntf', left, right, preferred_element_type=WIDE)  11.6 us
  transfers between devices with their start and end apart: 55, of which 18 were waited for; matrix products, arithmetic and copies ran while one was open for 45% of the time, Pallas kernels for 0%

profile of v1, /device:TPU:0, one launch (start us, length us, event | category | flops | bytes accessed | tf_op | source)
XLA Modules:
  0.0 568.4 jit_solution(5415568015059348239)
XLA Ops:
  2.9 3.0 collective-permute-start
  22.0 2.9 collective-permute-start.33
  26.2 5.0 collective-permute-start.4
  31.2 13.4 %collective-permute-done.32 = bf16[2,197,128]{2,1,0:T(8,128)(2,1)S(1)} collective-permute-done((bf16[2,197,128]{2,1,0:T(8,128)(2,1)S(1)}, bf16[2,197,128]{2,1,0:T(8,128)(2,1)S(1)}, u32[]{:S(2)}, u32[]{:S(2)}) %collective-permute-start.32) | collective-permute-done | bytes 100896 | tf_op jit(solution)/shard_map/ppermute | solution.py:26
  44.6 4.8 collective-permute-start.22
  52.8 18.5 %collective-permute-done.5 = bf16[384,256]{1,0:T(8,128)(2,1)S(1)} collective-permute-done((bf16[384,256]{1,0:T(8,128)(2,1)S(1)}, bf16[384,256]{1,0:T(8,128)(2,1)S(1)}, u32[]{:S(2)}, u32[]{:S(2)}) %collective-permute-start.5) | collective-permute-done | bytes 196640 | tf_op jit(solution)/shard_map/ppermute | solution.py:26
  71.3 5.2 collective-permute-start.23
  77.5 3.7 collective-permute-done.22
  82.7 14.4 %collective-permute-done.23 = bf16[512,256]{1,0:T(8,128)(2,1)S(1)} collective-permute-done((bf16[512,256]{1,0:T(8,128)(2,1)S(1)}, bf16[512,256]{1,0:T(8,128)(2,1)S(1)}, u32[]{:S(2)}, u32[]{:S(2)}) %collective-permute-start.23) | collective-permute-done | bytes 262176 | tf_op jit(solution)/shard_map/ppermute | solution.py:26
  108.2 3.9 reshape.753
  113.2 5.4 collective-permute-done.12
  125.5 15.6 %collective-permute-done.25 = bf16[4,512,256]{2,1,0:T(8,128)(2,1)} collective-permute-done((bf16[4,512,256]{2,1,0:T(8,128)(2,1)}, bf16[4,512,256]{2,1,0:T(8,128)(2,1)}, u32[]{:S(2)}, u32[]{:S(2)}) %collective-permute-start.25) | collective-permute-done | bytes 1048608 | tf_op jit(solution)/shard_map/ppermute | solution.py:35
  141.1 25.5 %collective-permute-done.18 = bf16[4,640,256]{2,1,0:T(8,128)(2,1)} collective-permute-done((bf16[4,640,256]{2,1,0:T(8,128)(2,1)}, bf16[4,640,256]{2,1,0:T(8,128)(2,1)}, u32[]{:S(2)}, u32[]{:S(2)}) %collective-permute-start.18) | collective-permute-done | bytes 1310752 | tf_op jit(solution)/shard_map/ppermute | solution.py:35
  192.8 5.7 %copy.256 = bf16[4,4,24,16,256]{4,1,3,0,2:T(4,128)(2,1)} copy(bf16[4,4,24,16,256]{4,3,2,1,0:T(8,128)(2,1)S(1)} %bitcast.512) | data formatting | bytes 6291456 | tf_op jit(solution)/shard_map/reshape | solution.py:225
  198.5 4.7 reshape.798
  203.6 4.3 fusion.9
  231.5 5.3 copy.271
  236.8 7.8 %reshape.803 = bf16[2048,1024,1]{1,0,2:T(8,128)(2,1)} reshape(bf16[4,512,4,256]{3,2,1,0:T(4,128)(2,1)} %copy.271) | data formatting | bytes 8388608 | tf_op jit(solution)/shard_map/reshape | solution.py:222
  244.6 5.2 copy.347
  249.8 6.5 %copy.272 = bf16[1024,2048]{1,0:T(8,128)(2,1)} copy(bf16[1024,2048]{0,1:T(8,128)(2,1)} %bitcast.503) | data formatting | bytes 8388608 | tf_op jit(solution)/shard_map/ntf,fa->nta/dot_general | solution.py:103
  258.8 5.2 copy.270
  264.0 7.8 %reshape.800 = bf16[2048,1024,1]{1,0,2:T(8,128)(2,1)} reshape(bf16[4,512,4,256]{3,2,1,0:T(4,128)(2,1)} %copy.270) | data formatting | bytes 8388608 | tf_op jit(solution)/shard_map/reshape | solution.py:222
  274.9 2.9 fusion.49
  277.9 8.8 %multiply_convert_fusion.1 = (bf16[2,197,2048]{2,1,0:T(8,128)(2,1)}, f32[2,197,2048]{2,1,0:T(8,128)S(1)}) fusion(f32[2,197,2048]{2,1,0:T(8,128)S(1)} %get-tuple-element.233, f32[2048]{0:T(1024)S(1)} %bitcast.597, u8[197,2048]{1,0:T(8,128)(4,1)S(1)} %get-tuple-element.116, u8[197,2048]{1,0:T(8,128)(4,1)S(1)} %get-tuple-element.115), kind=kLoop, calls=%fused_computation.42 | loop fusion | flops 57290752 | bytes 8884224 | tf_op jit(solution)/shard_map/convert_element_type | solution.py:245
  286.7 3.0 convert_reduce_fusion
  291.6 4.6 bitcast_convert_fusion.1
  299.1 7.9 %reshape.750 = bf16[4,512,4,256]{3,2,1,0:T(4,128)(2,1)} reshape(bf16[2048,1024]{1,0:T(8,128)(2,1)} %bitcast_convert_fusion.1) | data formatting | bytes 8388608 | tf_op jit(solution)/shard_map/reshape | solution.py:272
  307.0 6.0 %bitcast_convert_fusion = bf16[2048,1024]{1,0:T(8,128)(2,1)} fusion(bf16[2,197,2048]{2,1,0:T(8,128)(2,1)} %get-tuple-element.136, bf16[2,197,1024]{2,1,0:T(8,128)(2,1)} %reshape.737), kind=kOutput, calls=%fused_computation.10 | convolution fusion | flops 1654652928 | bytes 6615040 | tf_op jit(solution)/shard_map/ntf,nta->fa/dot_general | solution.py:107
  313.0 7.9 %reshape.751 = bf16[4,512,4,256]{3,2,1,0:T(4,128)(2,1)} reshape(bf16[2048,1024]{1,0:T(8,128)(2,1)} %bitcast_convert_fusion) | data formatting | bytes 8388608 | tf_op jit(solution)/shard_map/reshape | solution.py:272
  320.9 5.2 copy_bitcast_fusion
  339.7 3.9 convert_reduce_fusion.3
  362.9 3.6 fusion.127
  366.5 3.6 bitcast_convert_fusion.2
  378.0 6.2 %reshape.740 = bf16[24,4,16,4,256]{4,3,2,1,0:T(4,128)(2,1)} reshape(bf16[1536,1024]{1,0:T(8,128)(2,1)} %bitcast_convert_fusion.2) | data formatting | bytes 6291456 | tf_op jit(solution)/shard_map/reshape | solution.py:268
  386.8 3.1 collective-permute-start.29
  391.7 7.1 %collective-permute-done.29 = bf16[2,197,128]{2,1,0:T(8,128)(2,1)S(1)} collective-permute-done((bf16[2,197,128]{2,1,0:T(8,128)(2,1)S(1)}, bf16[2,197,128]{2,1,0:T(8,128)(2,1)S(1)}, u32[]{:S(2)}, u32[]{:S(2)}) %collective-permute-start.29) | collective-permute-done | bytes 100896 | tf_op jit(solution)/shard_map/ppermute | solution.py:26
  402.4 3.3 multiply_reduce_fusion.3
  408.8 4.0 multiply_add_fusion
  415.3 2.9 fusion.128
  422.7 10.8 %psum.7 = f32[1536]{0:T(1024)S(1)} all-reduce(f32[1536]{0:T(1024)S(1)} %add_add_fusion.1), channel_id=1, replica_groups=mesh['dp'=4,'row'=4,'col'=2] {'row'}, use_global_device_ids=true, to_apply=%region_19.20 | all-reduce | flops 1536 | bytes 12288 | tf_op jit(solution)/shard_map/psum | solution.py:299
  449.9 3.8 fusion.1
  454.8 18.9 %collective-permute-done.42 = bf16[4,512,256]{2,1,0:T(8,128)(2,1)S(1)} collective-permute-done((bf16[4,512,256]{2,1,0:T(8,128)(2,1)S(1)}, bf16[4,512,256]{2,1,0:T(8,128)(2,1)S(1)}, u32[]{:S(2)}, u32[]{:S(2)}) %collective-permute-start.42) | collective-permute-done | bytes 1048608 | tf_op jit(solution)/shard_map/ppermute | solution.py:35
  476.5 3.9 collective-permute-start.43
  489.8 6.3 %collective-permute-done.44 = bf16[512,256]{1,0:T(8,128)(2,1)S(1)} collective-permute-done((bf16[512,256]{1,0:T(8,128)(2,1)S(1)}, bf16[512,256]{1,0:T(8,128)(2,1)S(1)}, u32[]{:S(2)}, u32[]{:S(2)}) %collective-permute-start.44) | collective-permute-done | bytes 262176 | tf_op jit(solution)/shard_map/ppermute | solution.py:26
  498.5 16.3 %collective-permute-done.51 = bf16[4,1024,256]{2,1,0:T(8,128)(2,1)} collective-permute-done((bf16[4,1024,256]{2,1,0:T(8,128)(2,1)}, bf16[4,1024,256]{2,1,0:T(8,128)(2,1)}, u32[]{:S(2)}, u32[]{:S(2)}) %collective-permute-start.51) | collective-permute-done | bytes 2097184 | tf_op jit(solution)/shard_map/ppermute | solution.py:35
  514.8 3.3 add_convert_fusion
  522.9 8.3 %collective-permute-done.52 = bf16[1024,256]{1,0:T(8,128)(2,1)S(1)} collective-permute-done((bf16[1024,256]{1,0:T(8,128)(2,1)S(1)}, bf16[1024,256]{1,0:T(8,128)(2,1)S(1)}, u32[]{:S(2)}, u32[]{:S(2)}) %collective-permute-start.52) | collective-permute-done | bytes 524320 | tf_op jit(solution)/shard_map/ppermute | solution.py:26
  531.2 30.6 %collective-permute-done.53 = bf16[1024,256]{1,0:T(8,128)(2,1)S(1)} collective-permute-done((bf16[1024,256]{1,0:T(8,128)(2,1)S(1)}, bf16[1024,256]{1,0:T(8,128)(2,1)S(1)}, u32[]{:S(2)}, u32[]{:S(2)}) %collective-permute-start.53) | collective-permute-done | bytes 524320 | tf_op jit(solution)/shard_map/ppermute | solution.py:26
  (513 shorter events, 205.8 us)
Async XLA Ops:
  2.9 19.1 %collective-permute-start = (bf16[2,197,128]{2,1,0:T(8,128)(2,1)}, bf16[2,197,128]{2,1,0:T(8,128)(2,1)S(1)}, u32[]{:S(2)}, u32[]{:S(2)}) collective-permute-start(bf16[2,197,128]{2,1,0:T(8,128)(2,1)} %get-tuple-element.200), channel_id=1, source_target_pairs={{0,2},{2,4},{4,6},{6,0},{1,3},{3,5},{5,7},{7,1},{8,10},{10,12},{12... | collective-permute-start | bytes 302600 | tf_op jit(solution)/shard_map/ppermute | solution.py:26
  6.0 19.0 %collective-permute-start.1 = (bf16[2,197,128]{2,1,0:T(8,128)(2,1)}, bf16[2,197,128]{2,1,0:T(8,128)(2,1)S(1)}, u32[]{:S(2)}, u32[]{:S(2)}) collective-permute-start(bf16[2,197,128]{2,1,0:T(8,128)(2,1)} %get-tuple-element.199), channel_id=1, source_target_pairs={{0,4},{2,6},{4,0},{6,2},{1,5},{3,7},{5,1},{7,3},{8,12},{10,14},{12... | collective-permute-start | bytes 302600 | tf_op jit(solution)/shard_map/ppermute | solution.py:26
  17.0 9.2 %collective-permute-start.2 = (bf16[2,197,128]{2,1,0:T(8,128)(2,1)S(1)}, bf16[2,197,128]{2,1,0:T(8,128)(2,1)S(1)}, u32[]{:S(2)}, u32[]{:S(2)}) collective-permute-start(bf16[2,197,128]{2,1,0:T(8,128)(2,1)S(1)} %get-tuple-element.198), channel_id=1, source_target_pairs={{0,6},{2,0},{4,2},{6,4},{1,7},{3,1},{5,3},{7,5},{8,14},{10,8},{12,... | collective-permute-start | bytes 302600 | tf_op jit(solution)/shard_map/ppermute | solution.py:26
  19.8 11.4 %collective-permute-start.31 = (bf16[2,197,128]{2,1,0:T(8,128)(2,1)S(1)}, bf16[2,197,128]{2,1,0:T(8,128)(2,1)S(1)}, u32[]{:S(2)}, u32[]{:S(2)}) collective-permute-start(bf16[2,197,128]{2,1,0:T(8,128)(2,1)S(1)} %get-tuple-element.192), channel_id=1, source_target_pairs={{0,2},{2,4},{4,6},{6,0},{1,3},{3,5},{5,7},{7,1},{8,10},{10,12},{12... | collective-permute-start | bytes 302600 | tf_op jit(solution)/shard_map/ppermute | solution.py:26
  20.4 24.2 %collective-permute-start.32 = (bf16[2,197,128]{2,1,0:T(8,128)(2,1)S(1)}, bf16[2,197,128]{2,1,0:T(8,128)(2,1)S(1)}, u32[]{:S(2)}, u32[]{:S(2)}) collective-permute-start(bf16[2,197,128]{2,1,0:T(8,128)(2,1)S(1)} %get-tuple-element.191), channel_id=1, source_target_pairs={{0,4},{2,6},{4,0},{6,2},{1,5},{3,7},{5,1},{7,3},{8,12},{10,14},{12... | collective-permute-start | bytes 302600 | tf_op jit(solution)/shard_map/ppermute | solution.py:26
  22.0 22.6 %collective-permute-start.33 = (bf16[2,197,128]{2,1,0:T(8,128)(2,1)S(1)}, bf16[2,197,128]{2,1,0:T(8,128)(2,1)S(1)}, u32[]{:S(2)}, u32[]{:S(2)}) collective-permute-start(bf16[2,197,128]{2,1,0:T(8,128)(2,1)S(1)} %get-tuple-element.190), channel_id=1, source_target_pairs={{0,6},{2,0},{4,2},{6,4},{1,7},{3,1},{5,3},{7,5},{8,14},{10,8},{12,... | collective-permute-start | bytes 302600 | tf_op jit(solution)/shard_map/ppermute | solution.py:26
  24.9 46.4 %collective-permute-start.21 = (bf16[512,256]{1,0:T(8,128)(2,1)S(1)}, bf16[512,256]{1,0:T(8,128)(2,1)S(1)}, u32[]{:S(2)}, u32[]{:S(2)}) collective-permute-start(bf16[512,256]{1,0:T(8,128)(2,1)S(1)} %bitcast.547), channel_id=1, source_target_pairs={{0,2},{2,4},{4,6},{6,0},{1,3},{3,5},{5,7},{7,1},{8,10},{10,12},{12... | collective-permute-start | bytes 786440 | tf_op jit(solution)/shard_map/ppermute | solution.py:26
  26.2 24.1 %collective-permute-start.4 = (bf16[384,256]{1,0:T(8,128)(2,1)S(1)}, bf16[384,256]{1,0:T(8,128)(2,1)S(1)}, u32[]{:S(2)}, u32[]{:S(2)}) collective-permute-start(bf16[384,256]{1,0:T(8,128)(2,1)S(1)} %bitcast.535), channel_id=1, source_target_pairs={{0,2},{2,4},{4,6},{6,0},{1,3},{3,5},{5,7},{7,1},{8,10},{10,12},{12... | collective-permute-start | bytes 589832 | tf_op jit(solution)/shard_map/ppermute | solution.py:26
  31.2 40.1 %collective-permute-start.5 = (bf16[384,256]{1,0:T(8,128)(2,1)S(1)}, bf16[384,256]{1,0:T(8,128)(2,1)S(1)}, u32[]{:S(2)}, u32[]{:S(2)}) collective-permute-start(bf16[384,256]{1,0:T(8,128)(2,1)S(1)} %bitcast.536), channel_id=1, source_target_pairs={{0,4},{2,6},{4,0},{6,2},{1,5},{3,7},{5,1},{7,3},{8,12},{10,14},{12... | collective-permute-start | bytes 589832 | tf_op jit(solution)/shard_map/ppermute | solution.py:26
  44.6 26.7 %collective-permute-start.6 = (bf16[384,256]{1,0:T(8,128)(2,1)S(1)}, bf16[384,256]{1,0:T(8,128)(2,1)S(1)}, u32[]{:S(2)}, u32[]{:S(2)}) collective-permute-start(bf16[384,256]{1,0:T(8,128)(2,1)S(1)} %bitcast.537), channel_id=1, source_target_pairs={{0,6},{2,0},{4,2},{6,4},{1,7},{3,1},{5,3},{7,5},{8,14},{10,8},{12,... | collective-permute-start | bytes 589832 | tf_op jit(solution)/shard_map/ppermute | solution.py:26
  44.6 36.6 %collective-permute-start.22 = (bf16[512,256]{1,0:T(8,128)(2,1)S(1)}, bf16[512,256]{1,0:T(8,128)(2,1)S(1)}, u32[]{:S(2)}, u32[]{:S(2)}) collective-permute-start(bf16[512,256]{1,0:T(8,128)(2,1)S(1)} %bitcast.548), channel_id=1, source_target_pairs={{0,4},{2,6},{4,0},{6,2},{1,5},{3,7},{5,1},{7,3},{8,12},{10,14},{12... | collective-permute-start | bytes 786440 | tf_op jit(solution)/shard_map/ppermute | solution.py:26
  50.3 49.9 %collective-permute-start.14 = (bf16[640,256]{1,0:T(8,128)(2,1)S(1)}, bf16[640,256]{1,0:T(8,128)(2,1)S(1)}, u32[]{:S(2)}, u32[]{:S(2)}) collective-permute-start(bf16[640,256]{1,0:T(8,128)(2,1)S(1)} %get-tuple-element.202), channel_id=1, source_target_pairs={{0,2},{2,4},{4,6},{6,0},{1,3},{3,5},{5,7},{7,1},{8,10},{10,12},{12... | collective-permute-start | bytes 983048 | tf_op jit(solution)/shard_map/ppermute | solution.py:26
  71.3 30.3 %collective-permute-start.15 = (bf16[640,256]{1,0:T(8,128)(2,1)S(1)}, bf16[640,256]{1,0:T(8,128)(2,1)S(1)}, u32[]{:S(2)}, u32[]{:S(2)}) collective-permute-start(bf16[640,256]{1,0:T(8,128)(2,1)S(1)} %get-tuple-element.202), channel_id=1, source_target_pairs={{0,4},{2,6},{4,0},{6,2},{1,5},{3,7},{5,1},{7,3},{8,12},{10,14},{12... | collective-permute-start | bytes 983048 | tf_op jit(solution)/shard_map/ppermute | solution.py:26
  71.3 30.3 %collective-permute-start.16 = (bf16[640,256]{1,0:T(8,128)(2,1)S(1)}, bf16[640,256]{1,0:T(8,128)(2,1)S(1)}, u32[]{:S(2)}, u32[]{:S(2)}) collective-permute-start(bf16[640,256]{1,0:T(8,128)(2,1)S(1)} %get-tuple-element.202), channel_id=1, source_target_pairs={{0,6},{2,0},{4,2},{6,4},{1,7},{3,1},{5,3},{7,5},{8,14},{10,8},{12,... | collective-permute-start | bytes 983048 | tf_op jit(solution)/shard_map/ppermute | solution.py:26
  71.3 25.8 %collective-permute-start.23 = (bf16[512,256]{1,0:T(8,128)(2,1)S(1)}, bf16[512,256]{1,0:T(8,128)(2,1)S(1)}, u32[]{:S(2)}, u32[]{:S(2)}) collective-permute-start(bf16[512,256]{1,0:T(8,128)(2,1)S(1)} %bitcast.549), channel_id=1, source_target_pairs={{0,6},{2,0},{4,2},{6,4},{1,7},{3,1},{5,3},{7,5},{8,14},{10,8},{12,... | collective-permute-start | bytes 786440 | tf_op jit(solution)/shard_map/ppermute | solution.py:26
  81.3 22.8 %collective-permute-start.3 = (bf16[4,2,197,128]{3,2,1,0:T(8,128)(2,1)S(1)}, bf16[4,2,197,128]{3,2,1,0:T(8,128)(2,1)S(1)}, u32[]{:S(2)}, u32[]{:S(2)}) collective-permute-start(bf16[4,2,197,128]{3,2,1,0:T(8,128)(2,1)S(1)} %pad_maximum_fusion.17), channel_id=1, source_target_pairs={{0,1},{1,0},{2,3},{3,2},{4,5},{5,4},{6,7},{7,6},{8,9},{9,8},{10,11... | collective-permute-start | bytes 1210376 | tf_op jit(solution)/shard_map/ppermute | solution.py:30
  97.1 21.5 %collective-permute-start.12 = (bf16[4,400,256]{2,1,0:T(8,128)(2,1)}, bf16[4,400,256]{2,1,0:T(8,128)(2,1)}, u32[]{:S(2)}, u32[]{:S(2)}) collective-permute-start(bf16[4,400,256]{2,1,0:T(8,128)(2,1)} %pad_maximum_fusion.15), channel_id=1, source_target_pairs={{0,16},{8,24},{16,0},{24,8},{1,17},{9,25},{17,1},{25,9},{2,18},{10... | collective-permute-start | bytes 2457608 | tf_op jit(solution)/shard_map/ppermute | solution.py:35
  100.2 11.9 %collective-permute-start.34 = (bf16[4,2,197,128]{3,2,1,0:T(8,128)(2,1)}, bf16[4,2,197,128]{3,2,1,0:T(8,128)(2,1)}, u32[]{:S(2)}, u32[]{:S(2)}) collective-permute-start(bf16[4,2,197,128]{3,2,1,0:T(8,128)(2,1)} %pad_maximum_fusion.19), channel_id=1, source_target_pairs={{0,1},{1,0},{2,3},{3,2},{4,5},{5,4},{6,7},{7,6},{8,9},{9,8},{10,11... | collective-permute-start | bytes 1210376 | tf_op jit(solution)/shard_map/ppermute | solution.py:30
  101.6 23.4 %collective-permute-start.11 = (bf16[4,400,256]{2,1,0:T(8,128)(2,1)}, bf16[4,400,256]{2,1,0:T(8,128)(2,1)}, u32[]{:S(2)}, u32[]{:S(2)}) collective-permute-start(bf16[4,400,256]{2,1,0:T(8,128)(2,1)} %pad_maximum_fusion.15), channel_id=1, source_target_pairs={{0,8},{8,0},{16,24},{24,16},{1,9},{9,1},{17,25},{25,17},{2,10},{10... | collective-permute-start | bytes 2457608 | tf_op jit(solution)/shard_map/ppermute | solution.py:35
  101.7 39.5 %collective-permute-start.25 = (bf16[4,512,256]{2,1,0:T(8,128)(2,1)}, bf16[4,512,256]{2,1,0:T(8,128)(2,1)}, u32[]{:S(2)}, u32[]{:S(2)}) collective-permute-start(bf16[4,512,256]{2,1,0:T(8,128)(2,1)} %get-tuple-element.171), channel_id=1, source_target_pairs={{0,16},{8,24},{16,0},{24,8},{1,17},{9,25},{17,1},{25,9},{2,18},{10... | collective-permute-start | bytes 3145736 | tf_op jit(solution)/shard_map/ppermute | solution.py:35
  104.0 62.6 %collective-permute-start.18 = (bf16[4,640,256]{2,1,0:T(8,128)(2,1)}, bf16[4,640,256]{2,1,0:T(8,128)(2,1)}, u32[]{:S(2)}, u32[]{:S(2)}) collective-permute-start(bf16[4,640,256]{2,1,0:T(8,128)(2,1)} %get-tuple-element.156), channel_id=1, source_target_pairs={{0,16},{8,24},{16,0},{24,8},{1,17},{9,25},{17,1},{25,9},{2,18},{10... | collective-permute-start | bytes 3932168 | tf_op jit(solution)/shard_map/ppermute | solution.py:35
  112.1 117.0 %collective-permute-start.24 = (bf16[4,512,256]{2,1,0:T(8,128)(2,1)}, bf16[4,512,256]{2,1,0:T(8,128)(2,1)}, u32[]{:S(2)}, u32[]{:S(2)}) collective-permute-start(bf16[4,512,256]{2,1,0:T(8,128)(2,1)} %get-tuple-element.171), channel_id=1, source_target_pairs={{0,8},{8,0},{16,24},{24,16},{1,9},{9,1},{17,25},{25,17},{2,10},{10... | collective-permute-start | bytes 3145736 | tf_op jit(solution)/shard_map/ppermute | solution.py:35
  118.6 48.0 %collective-permute-start.13 = (bf16[4,400,256]{2,1,0:T(8,128)(2,1)}, bf16[4,400,256]{2,1,0:T(8,128)(2,1)S(1)}, u32[]{:S(2)}, u32[]{:S(2)}) collective-permute-start(bf16[4,400,256]{2,1,0:T(8,128)(2,1)} %collective-permute-done.12), channel_id=1, source_target_pairs={{0,8},{8,0},{16,24},{24,16},{1,9},{9,1},{17,25},{25,17},{2,10},{10... | collective-permute-start | bytes 2457608 | tf_op jit(solution)/shard_map/ppermute | solution.py:35
  125.0 91.4 %collective-permute-start.17 = (bf16[4,640,256]{2,1,0:T(8,128)(2,1)}, bf16[4,640,256]{2,1,0:T(8,128)(2,1)}, u32[]{:S(2)}, u32[]{:S(2)}) collective-permute-start(bf16[4,640,256]{2,1,0:T(8,128)(2,1)} %get-tuple-element.156), channel_id=1, source_target_pairs={{0,8},{8,0},{16,24},{24,16},{1,9},{9,1},{17,25},{25,17},{2,10},{10... | collective-permute-start | bytes 3932168 | tf_op jit(solution)/shard_map/ppermute | solution.py:35
  141.1 88.0 %collective-permute-start.26 = (bf16[4,512,256]{2,1,0:T(8,128)(2,1)}, bf16[4,512,256]{2,1,0:T(8,128)(2,1)}, u32[]{:S(2)}, u32[]{:S(2)}) collective-permute-start(bf16[4,512,256]{2,1,0:T(8,128)(2,1)} %collective-permute-done.25), channel_id=1, source_target_pairs={{0,8},{8,0},{16,24},{24,16},{1,9},{9,1},{17,25},{25,17},{2,10},{10... | collective-permute-start | bytes 3145736 | tf_op jit(solution)/shard_map/ppermute | solution.py:35
  166.6 49.8 %collective-permute-start.19 = (bf16[4,640,256]{2,1,0:T(8,128)(2,1)}, bf16[4,640,256]{2,1,0:T(8,128)(2,1)}, u32[]{:S(2)}, u32[]{:S(2)}) collective-permute-start(bf16[4,640,256]{2,1,0:T(8,128)(2,1)} %collective-permute-done.18), channel_id=1, source_target_pairs={{0,8},{8,0},{16,24},{24,16},{1,9},{9,1},{17,25},{25,17},{2,10},{10... | collective-permute-start | bytes 3932168 | tf_op jit(solution)/shard_map/ppermute | solution.py:35
  226.7 45.1 %collective-permute-start.20 = (bf16[2,197,1024]{2,0,1:T(2,128)(2,1)}, bf16[2,197,1024]{2,0,1:T(2,128)(2,1)}, u32[]{:S(2)}, u32[]{:S(2)}) collective-permute-start(bf16[2,197,1024]{2,0,1:T(2,128)(2,1)} %copy.266), channel_id=1, source_target_pairs={{0,1},{1,0},{2,3},{3,2},{4,5},{5,4},{6,7},{7,6},{8,9},{9,8},{10,11... | collective-permute-start | bytes 2420744 | tf_op jit(solution)/shard_map/ppermute | solution.py:30
  297.9 39.2 %collective-permute-start.35 = (bf16[2,197,1024]{2,0,1:T(2,128)(2,1)}, bf16[2,197,1024]{2,0,1:T(2,128)(2,1)}, u32[]{:S(2)}, u32[]{:S(2)}) collective-permute-start(bf16[2,197,1024]{2,0,1:T(2,128)(2,1)} %copy.281), channel_id=1, source_target_pairs={{0,1},{1,0},{2,3},{3,2},{4,5},{5,4},{6,7},{7,6},{8,9},{9,8},{10,11... | collective-permute-start | bytes 2420744 | tf_op jit(solution)/shard_map/ppermute | solution.py:30
  332.1 117.8 %collective-permute-start.50 = (bf16[4,1024,256]{2,1,0:T(8,128)(2,1)}, bf16[4,1024,256]{2,1,0:T(8,128)(2,1)}, u32[]{:S(2)}, u32[]{:S(2)}) collective-permute-start(bf16[4,1024,256]{2,1,0:T(8,128)(2,1)} %get-tuple-element.141), channel_id=1, source_target_pairs={{0,8},{8,0},{16,24},{24,16},{1,9},{9,1},{17,25},{25,17},{2,10},{10... | collective-permute-start | bytes 6291464 | tf_op jit(solution)/shard_map/ppermute | solution.py:35
  335.7 34.4 %collective-permute-start.27 = (bf16[2,197,4,128]{3,1,2,0:T(8,128)(2,1)}, bf16[2,197,4,128]{3,1,2,0:T(8,128)(2,1)}, u32[]{:S(2)}, u32[]{:S(2)}) collective-permute-start(bf16[2,197,4,128]{3,1,2,0:T(8,128)(2,1)} %fusion.63), channel_id=1, source_target_pairs={{0,1},{1,0},{2,3},{3,2},{4,5},{5,4},{6,7},{7,6},{8,9},{9,8},{10,11... | collective-permute-start | bytes 1210376 | tf_op jit(solution)/shard_map/ppermute | solution.py:30
  359.7 42.7 %collective-permute-start.36 = (bf16[2,197,1024]{2,0,1:T(2,128)(2,1)}, bf16[2,197,1024]{2,0,1:T(2,128)(2,1)}, u32[]{:S(2)}, u32[]{:S(2)}) collective-permute-start(bf16[2,197,1024]{2,0,1:T(2,128)(2,1)} %copy.289), channel_id=1, source_target_pairs={{0,1},{1,0},{2,3},{3,2},{4,5},{5,4},{6,7},{7,6},{8,9},{9,8},{10,11... | collective-permute-start | bytes 2420744 | tf_op jit(solution)/shard_map/ppermute | solution.py:30
  386.8 11.9 %collective-permute-start.29 = (bf16[2,197,128]{2,1,0:T(8,128)(2,1)S(1)}, bf16[2,197,128]{2,1,0:T(8,128)(2,1)S(1)}, u32[]{:S(2)}, u32[]{:S(2)}) collective-permute-start(bf16[2,197,128]{2,1,0:T(8,128)(2,1)S(1)} %get-tuple-element.196), channel_id=1, source_target_pairs={{0,4},{2,6},{4,0},{6,2},{1,5},{3,7},{5,1},{7,3},{8,12},{10,14},{12... | collective-permute-start | bytes 302600 | tf_op jit(solution)/shard_map/ppermute | solution.py:26
  390.0 8.8 %collective-permute-start.30 = (bf16[2,197,128]{2,1,0:T(8,128)(2,1)S(1)}, bf16[2,197,128]{2,1,0:T(8,128)(2,1)S(1)}, u32[]{:S(2)}, u32[]{:S(2)}) collective-permute-start(bf16[2,197,128]{2,1,0:T(8,128)(2,1)S(1)} %get-tuple-element.195), channel_id=1, source_target_pairs={{0,2},{2,4},{4,6},{6,0},{1,3},{3,5},{5,7},{7,1},{8,10},{10,12},{12... | collective-permute-start | bytes 302600 | tf_op jit(solution)/shard_map/ppermute | solution.py:26
  391.7 106.8 %collective-permute-start.49 = (bf16[4,1024,256]{2,1,0:T(8,128)(2,1)}, bf16[4,1024,256]{2,1,0:T(8,128)(2,1)}, u32[]{:S(2)}, u32[]{:S(2)}) collective-permute-start(bf16[4,1024,256]{2,1,0:T(8,128)(2,1)} %get-tuple-element.140), channel_id=1, source_target_pairs={{0,8},{8,0},{16,24},{24,16},{1,9},{9,1},{17,25},{25,17},{2,10},{10... | collective-permute-start | bytes 6291464 | tf_op jit(solution)/shard_map/ppermute | solution.py:35
  398.7 47.2 %collective-permute-start.41 = (bf16[4,512,256]{2,1,0:T(8,128)(2,1)}, bf16[4,512,256]{2,1,0:T(8,128)(2,1)}, u32[]{:S(2)}, u32[]{:S(2)}) collective-permute-start(bf16[4,512,256]{2,1,0:T(8,128)(2,1)} %get-tuple-element.143), channel_id=1, source_target_pairs={{0,8},{8,0},{16,24},{24,16},{1,9},{9,1},{17,25},{25,17},{2,10},{10... | collective-permute-start | bytes 3145736 | tf_op jit(solution)/shard_map/ppermute | solution.py:35
  407.5 10.8 %collective-permute-start.47 = (f32[1536]{0:T(1024)S(1)}, f32[1536]{0:T(1024)S(1)}, u32[]{:S(2)}, u32[]{:S(2)}) collective-permute-start(f32[1536]{0:T(1024)S(1)} %get-tuple-element.126), channel_id=1, source_target_pairs={{0,8},{8,0},{16,24},{24,16},{1,9},{9,1},{17,25},{25,17},{2,10},{10... | collective-permute-start | bytes 18440 | tf_op jit(solution)/shard_map/ppermute | solution.py:35
  408.0 12.5 %collective-permute-start.46 = (f32[1536]{0:T(1024)S(1)}, f32[1536]{0:T(1024)S(1)}, u32[]{:S(2)}, u32[]{:S(2)}) collective-permute-start(f32[1536]{0:T(1024)S(1)} %get-tuple-element.125), channel_id=1, source_target_pairs={{0,8},{8,0},{16,24},{24,16},{1,9},{9,1},{17,25},{25,17},{2,10},{10... | collective-permute-start | bytes 18440 | tf_op jit(solution)/shard_map/ppermute | solution.py:35
  420.5 34.3 %collective-permute-start.40 = (bf16[4,512,256]{2,1,0:T(8,128)(2,1)}, bf16[4,512,256]{2,1,0:T(8,128)(2,1)}, u32[]{:S(2)}, u32[]{:S(2)}) collective-permute-start(bf16[4,512,256]{2,1,0:T(8,128)(2,1)} %get-tuple-element.142), channel_id=1, source_target_pairs={{0,8},{8,0},{16,24},{24,16},{1,9},{9,1},{17,25},{25,17},{2,10},{10... | collective-permute-start | bytes 3145736 | tf_op jit(solution)/shard_map/ppermute | solution.py:35
  422.0 54.5 %collective-permute-start.37 = (bf16[2,197,128]{2,1,0:T(8,128)(2,1)}, bf16[2,197,128]{2,1,0:T(8,128)(2,1)S(1)}, u32[]{:S(2)}, u32[]{:S(2)}) collective-permute-start(bf16[2,197,128]{2,1,0:T(8,128)(2,1)} %get-tuple-element.186), channel_id=1, source_target_pairs={{0,6},{2,0},{4,2},{6,4},{1,7},{3,1},{5,3},{7,5},{8,14},{10,8},{12,... | collective-permute-start | bytes 302600 | tf_op jit(solution)/shard_map/ppermute | solution.py:26
  447.6 26.2 %collective-permute-start.42 = (bf16[4,512,256]{2,1,0:T(8,128)(2,1)S(1)}, bf16[4,512,256]{2,1,0:T(8,128)(2,1)S(1)}, u32[]{:S(2)}, u32[]{:S(2)}) collective-permute-start(bf16[4,512,256]{2,1,0:T(8,128)(2,1)S(1)} %fusion.18), channel_id=1, source_target_pairs={{0,16},{8,24},{16,0},{24,8},{1,17},{9,25},{17,1},{25,9},{2,18},{10... | collective-permute-start | bytes 3145736 | tf_op jit(solution)/shard_map/ppermute | solution.py:35
  453.7 61.1 %collective-permute-start.51 = (bf16[4,1024,256]{2,1,0:T(8,128)(2,1)}, bf16[4,1024,256]{2,1,0:T(8,128)(2,1)}, u32[]{:S(2)}, u32[]{:S(2)}) collective-permute-start(bf16[4,1024,256]{2,1,0:T(8,128)(2,1)} %fusion.1), channel_id=1, source_target_pairs={{0,16},{8,24},{16,0},{24,8},{1,17},{9,25},{17,1},{25,9},{2,18},{10... | collective-permute-start | bytes 6291464 | tf_op jit(solution)/shard_map/ppermute | solution.py:35
  454.8 25.5 %collective-permute-start.38 = (bf16[2,197,128]{2,1,0:T(8,128)(2,1)S(1)}, bf16[2,197,128]{2,1,0:T(8,128)(2,1)S(1)}, u32[]{:S(2)}, u32[]{:S(2)}) collective-permute-start(bf16[2,197,128]{2,1,0:T(8,128)(2,1)S(1)} %copy-done.72), channel_id=1, source_target_pairs={{0,4},{2,6},{4,0},{6,2},{1,5},{3,7},{5,1},{7,3},{8,12},{10,14},{12... | collective-permute-start | bytes 302600 | tf_op jit(solution)/shard_map/ppermute | solution.py:26
  476.5 13.3 %collective-permute-start.43 = (bf16[512,256]{1,0:T(8,128)(2,1)S(1)}, bf16[512,256]{1,0:T(8,128)(2,1)S(1)}, u32[]{:S(2)}, u32[]{:S(2)}) collective-permute-start(bf16[512,256]{1,0:T(8,128)(2,1)S(1)} %get-tuple-element.167), channel_id=1, source_target_pairs={{0,6},{2,0},{4,2},{6,4},{1,7},{3,1},{5,3},{7,5},{8,14},{10,8},{12,... | collective-permute-start | bytes 786440 | tf_op jit(solution)/shard_map/ppermute | solution.py:26
  480.3 15.8 %collective-permute-start.44 = (bf16[512,256]{1,0:T(8,128)(2,1)S(1)}, bf16[512,256]{1,0:T(8,128)(2,1)S(1)}, u32[]{:S(2)}, u32[]{:S(2)}) collective-permute-start(bf16[512,256]{1,0:T(8,128)(2,1)S(1)} %get-tuple-element.169), channel_id=1, source_target_pairs={{0,4},{2,6},{4,0},{6,2},{1,5},{3,7},{5,1},{7,3},{8,12},{10,14},{12... | collective-permute-start | bytes 786440 | tf_op jit(solution)/shard_map/ppermute | solution.py:26
  481.6 14.6 %collective-permute-start.45 = (bf16[512,256]{1,0:T(8,128)(2,1)S(1)}, bf16[512,256]{1,0:T(8,128)(2,1)S(1)}, u32[]{:S(2)}, u32[]{:S(2)}) collective-permute-start(bf16[512,256]{1,0:T(8,128)(2,1)S(1)} %get-tuple-element.168), channel_id=1, source_target_pairs={{0,2},{2,4},{4,6},{6,0},{1,3},{3,5},{5,7},{7,1},{8,10},{10,12},{12... | collective-permute-start | bytes 786440 | tf_op jit(solution)/shard_map/ppermute | solution.py:26
  518.3 12.9 %collective-permute-start.52 = (bf16[1024,256]{1,0:T(8,128)(2,1)S(1)}, bf16[1024,256]{1,0:T(8,128)(2,1)S(1)}, u32[]{:S(2)}, u32[]{:S(2)}) collective-permute-start(bf16[1024,256]{1,0:T(8,128)(2,1)S(1)} %get-tuple-element.146), channel_id=1, source_target_pairs={{0,6},{2,0},{4,2},{6,4},{1,7},{3,1},{5,3},{7,5},{8,14},{10,8},{12,... | collective-permute-start | bytes 1572872 | tf_op jit(solution)/shard_map/ppermute | solution.py:26
  518.8 43.0 %collective-permute-start.53 = (bf16[1024,256]{1,0:T(8,128)(2,1)S(1)}, bf16[1024,256]{1,0:T(8,128)(2,1)S(1)}, u32[]{:S(2)}, u32[]{:S(2)}) collective-permute-start(bf16[1024,256]{1,0:T(8,128)(2,1)S(1)} %get-tuple-element.148), channel_id=1, source_target_pairs={{0,4},{2,6},{4,0},{6,2},{1,5},{3,7},{5,1},{7,3},{8,12},{10,14},{12... | collective-permute-start | bytes 1572872 | tf_op jit(solution)/shard_map/ppermute | solution.py:26
  520.0 41.9 %collective-permute-start.54 = (bf16[1024,256]{1,0:T(8,128)(2,1)S(1)}, bf16[1024,256]{1,0:T(8,128)(2,1)S(1)}, u32[]{:S(2)}, u32[]{:S(2)}) collective-permute-start(bf16[1024,256]{1,0:T(8,128)(2,1)S(1)} %get-tuple-element.147), channel_id=1, source_target_pairs={{0,2},{2,4},{4,6},{6,0},{1,3},{3,5},{5,7},{7,1},{8,10},{10,12},{12... | collective-permute-start | bytes 1572872 | tf_op jit(solution)/shard_map/ppermute | solution.py:26
  (110 other events, 1186.9 us)

commit v2 on v1

v2 whole, which is shorter than its diff:
```python
import functools
import math

import jax
import jax.numpy as jnp
from jax import lax
from jax.experimental import pallas as pl
from jax.experimental.pallas import tpu as pltpu
from jax.sharding import PartitionSpec as P

HD = 64
SEQ = 197
PAD = 208
STEP = 10

norm_eps = 1e-06
beta_first = 0.9
beta_second = 0.999
learn_rate = 0.01
weight_decay = 0.05
adam_eps = 1e-08
grad_gain = 32.0

LOW = jnp.bfloat16
WIDE = jnp.float32


def turn(values, shift):
    count = lax.axis_size("row")
    return lax.ppermute(values, "row", [(i, (i + shift) % count) for i in range(count)])


def swap_col(values):
    return lax.ppermute(values, "col", [(0, 1), (1, 0)])


def swap_dp(values, bit):
    count = lax.axis_size("dp")
    return lax.ppermute(values, "dp", [(i, i ^ bit) for i in range(count)])


def dp_bits():
    bits = []
    bit = 1
    while bit < lax.axis_size("dp"):
        bits.append(bit)
        bit *= 2
    return bits


def gather_row(values):
    return [values] + [turn(values, k) for k in range(1, lax.axis_size("row"))]


def gather_dp(values):
    blocks = {0: values}
    for bit in reversed(dp_bits()):
        for place in list(blocks):
            blocks[place ^ bit] = swap_dp(blocks[place], bit)
    return [blocks[d] for d in range(len(blocks))]


def scatter_dp(blocks, kind):
    held = dict(enumerate(blocks))
    for bit in dp_bits():
        for place in [d for d in held if not d & bit]:
            came = swap_dp(held.pop(place ^ bit), bit)
            held[place] = (held[place].astype(WIDE) + came.astype(WIDE)).astype(kind)
    return held[0]


def scatter_row(blocks):
    total = blocks[0].astype(WIDE)
    for k in range(1, len(blocks)):
        total = total + turn(blocks[k], -k).astype(WIDE)
    return total


def xor_order(values, axis):
    mine = lax.axis_index("dp")
    shape = values.shape
    for bit in dp_bits():
        split = values.reshape(shape[:axis] + (shape[axis] // (2 * bit), 2, bit) + shape[axis + 1 :])
        flipped = jnp.flip(split, axis + 1)
        values = jnp.where((mine & bit) > 0, flipped, split).reshape(shape)
    return values


def adam_step(weight_old, gradient, moments, decay_on):
    first_moment = beta_first * moments[0] + (1.0 - beta_first) * gradient
    second_moment = beta_second * moments[1] + (1.0 - beta_second) * gradient * gradient
    first_hat = first_moment / (1.0 - beta_first**STEP)
    second_hat = second_moment / (1.0 - beta_second**STEP)
    change = -learn_rate * (first_hat / (jnp.sqrt(second_hat) + adam_eps) + decay_on * weight_old)
    return (change, jnp.stack([first_moment, second_moment]))


def dot_nt(left, right):
    return lax.dot_general(left, right, (((1,), (1,)), ((), ())), preferred_element_type=WIDE)


def dot_nn(left, right):
    return lax.dot_general(left, right, (((1,), (0,)), ((), ())), preferred_element_type=WIDE)


def dot_tn(left, right):
    return lax.dot_general(left, right, (((0,), (0,)), ((), ())), preferred_element_type=WIDE)


def moments_of(stream):
    center = jnp.mean(stream, axis=-1, keepdims=True)
    offset = stream - center
    inv_std = lax.rsqrt(jnp.mean(offset * offset, axis=-1, keepdims=True) + norm_eps)
    return offset * inv_std, inv_std


def norm_backward(grad_norm, scaled, inv_std, gain):
    weighted = grad_norm * gain
    return inv_std * (
        weighted
        - jnp.mean(weighted, axis=-1, keepdims=True)
        - scaled * jnp.mean(weighted * scaled, axis=-1, keepdims=True)
    )


def lay_strips(low_col, near, far, rows):
    pieces = []
    for k in range(rows):
        mine, other = near(k), far(k)
        pieces.append(jnp.where(low_col, mine, other))
        pieces.append(jnp.where(low_col, other, mine))
    return jnp.concatenate(pieces, axis=1)


def lay_rows(blocks, rows, first, count):
    parts = []
    for k in range(rows):
        total = blocks[0][k, first:, :].astype(WIDE)
        for block in blocks[1:]:
            total = total + block[k, first:, :].astype(WIDE)
        parts.append(total[:count])
    return jnp.concatenate(parts, axis=1)


def lay_heads(target, blocks, me, groups, rows):
    own = HD // len(blocks)
    for k in range(rows):
        for d, block in enumerate(blocks):
            place = me ^ d if len(blocks) > 1 else 0
            for g in range(groups):
                at = g * HD + place * own
                if len(blocks) > 1:
                    at = pl.multiple_of(at, own)
                target[k, pl.ds(at, own), :] = block[k, g * own : (g + 1) * own, :]


def soft(scores):
    lane = lax.broadcasted_iota(jnp.int32, scores.shape, 1)
    scores = jnp.where(lane < SEQ, scores * (1.0 / math.sqrt(HD)), -1e30)
    raised = jnp.exp(scores - jnp.max(scores, axis=-1, keepdims=True))
    return raised * (1.0 / jnp.sum(raised, axis=-1, keepdims=True))


def first_kernel(spec, pos, near, far, *refs):
    n, rows, heads, width = spec
    qkv, out = refs[:n], refs[n : 2 * n]
    vec_o, x_o, normed_o, packed_o, att_o, part_o, qkv_s, out_s = refs[2 * n :]
    low_col, me = pos[0] == 0, pos[1]
    count = 3 * heads * HD // n
    vec = lay_rows(qkv, rows, count, 6)
    vec_o[0:6, :] = vec
    small = qkv[0][0, count:, :].astype(WIDE)
    for d in range(1, n):
        small = small + qkv[d][0, count:, :].astype(WIDE)
    lay_heads(qkv_s, qkv, me, 3 * heads, rows)
    lay_heads(out_s, out, me, heads, rows)
    stream = lay_strips(low_col, lambda k: near[k, 0], lambda k: far[k, 0], rows)
    x_o[...] = stream
    scaled, _ = moments_of(stream.astype(WIDE))
    normed = (scaled * vec[0:1] + vec[1:2]).astype(LOW)
    normed_o[...] = normed
    span = heads * HD
    lines = span // width
    for part in range(3):
        total = dot_nt(normed[:, :width], qkv_s[0, part * span : (part + 1) * span, :])
        for k in range(1, rows):
            total = total + dot_nt(normed[:, k * width : (k + 1) * width], qkv_s[k, part * span : (part + 1) * span, :])
        if part != 1:
            line = 6 + (lines if part == 2 else 0)
            total = total + jnp.concatenate([small[line + i : line + i + 1] for i in range(lines)], axis=1)
        packed_o[:, part * span : (part + 1) * span] = total.astype(LOW)
    two = 2 * HD
    lane = lax.broadcasted_iota(jnp.int32, (1, two), 1)
    for pair in range(heads // 2):
        at = pair * two
        queries = packed_o[:, at : at + two]
        key_rows = packed_o[:, span + at : span + at + two]
        values = packed_o[:, 2 * span + at : 2 * span + at + two]
        halves = []
        for side in range(2):
            mask = (lane < HD) if side == 0 else (lane >= HD)
            probs = soft(dot_nt(jnp.where(mask, queries, jnp.zeros_like(queries)), key_rows))
            halves.append(dot_nn(probs.astype(LOW), values))
        att_o[:, at : at + two] = jnp.where(lane < HD, halves[0], halves[1]).astype(LOW)
    for k in range(rows):
        part_o[:, k * width : (k + 1) * width] = dot_nn(att_o[...], out_s[k]).astype(LOW)


def gelu_both(values):
    tail = 0.5 * (1.0 + lax.erf(values * (1.0 / math.sqrt(2.0))))
    bell = jnp.exp(values * values * -0.5) * (1.0 / math.sqrt(2.0 * math.pi))
    return values * tail, tail + values * bell


def feed_kernel(spec, pos, vec, small, x, part, came, near, far, *refs):
    n, rows, groups, width, block = spec
    up, down = refs[:n], refs[n : 2 * n]
    (mid_o, normed_o, dy_o, units_o, hid_o, unit_sum_o, dy_sum_o, top_o, far_o, back_o, mixed_s, back_s) = refs[2 * n :]
    low_col, me = pos[0] == 0, pos[1]
    step = pl.program_id(0)

    @pl.when(step == 0)
    def _():
        dy = lay_strips(low_col, lambda k: near[k, 0], lambda k: far[k, 0], rows)
        dy_o[...] = dy
        dy_sum_o[...] = jnp.sum(dy.astype(WIDE), axis=0, keepdims=True)
        middle = x[...].astype(WIDE) + (part[...].astype(WIDE) + came[...].astype(WIDE) + vec[2:3, :])
        mid_o[...] = middle
        scaled, _ = moments_of(middle)
        normed_o[...] = (scaled * vec[3:4, :] + vec[4:5, :]).astype(LOW)
        mixed_s[...] = jnp.zeros_like(mixed_s)
        back_s[...] = jnp.zeros_like(back_s)

    def cols(ref, k):
        return ref[:, k * width : (k + 1) * width]

    up_rows = [jnp.concatenate([w[k] for w in up], axis=0) for k in range(rows)]
    down_rows = [jnp.concatenate([w[k] for w in down], axis=0) for k in range(rows)]
    hidden = dot_nt(cols(normed_o, 0), up_rows[0])
    for k in range(1, rows):
        hidden = hidden + dot_nt(cols(normed_o, k), up_rows[k])
    hidden = hidden + small[0]
    active, slope = gelu_both(hidden)
    active = active.astype(LOW)
    units_o[...] = active
    grad = dot_nt(cols(dy_o, 0), down_rows[0])
    for k in range(1, rows):
        grad = grad + dot_nt(cols(dy_o, k), down_rows[k])
    grad = (grad * slope).astype(LOW)
    hid_o[...] = grad
    unit_sum_o[...] = jnp.sum(grad.astype(WIDE), axis=0, keepdims=True)
    for k in range(rows):
        at = slice(k * width, (k + 1) * width)
        mixed_s[:, at] += dot_nn(active, down_rows[k])
        back_s[:, at] += dot_nn(grad, up_rows[k])

    @pl.when(step == pl.num_programs(0) - 1)
    def _():
        back_o[...] = back_s[...].astype(LOW)
        half = width // 2
        for k in range(rows):
            left, right = slice(k * width, k * width + half), slice(k * width + half, (k + 1) * width)
            base = mid_o[...] + vec[5:6, :]
            top_l, top_r = mixed_s[:, left] + base[:, left], mixed_s[:, right] + base[:, right]
            top_o[k] = jnp.where(low_col, top_l, top_r)
            far_o[k] = jnp.where(low_col, mixed_s[:, right], mixed_s[:, left]).astype(LOW)


def feed_grad_kernel(spec, *refs):
    n, rows, width = spec
    left, right, outs = refs[0:2], refs[2:4], refs[4:]
    total = dot_tn(left[0][...], right[0][...]) + dot_tn(left[1][...], right[1][...])
    block = total.shape[0] // n
    for d in range(n):
        for k in range(rows):
            outs[d][k] = total[d * block : (d + 1) * block, k * width : (k + 1) * width].astype(LOW)


def second_kernel(spec, pos, vec, mid, back, came, dy, packed, *refs):
    n, rows, heads, width = spec
    qkv, out = refs[:n], refs[n : 2 * n]
    dmid_o, dz_o, dpacked_o, back_o, sums_o, psum_o, qkv_s, out_s, datt_s = refs[2 * n :]
    me = pos[1]
    lay_heads(qkv_s, qkv, me, 3 * heads, rows)
    lay_heads(out_s, out, me, heads, rows)
    grad_norm = back[...].astype(WIDE) + came[...].astype(WIDE)
    scaled, inv_std = moments_of(mid[...])
    dmid = dy[...].astype(WIDE) + norm_backward(grad_norm, scaled, inv_std, vec[3:4, :])
    dmid_o[...] = dmid
    dz = dmid.astype(LOW)
    dz_o[...] = dz
    sums_o[0:1, :] = jnp.sum(dz.astype(WIDE), axis=0, keepdims=True)
    sums_o[1:2, :] = jnp.sum(grad_norm * scaled, axis=0, keepdims=True)
    sums_o[2:3, :] = jnp.sum(grad_norm, axis=0, keepdims=True)
    total = dot_nt(dz[:, :width], out_s[0])
    for k in range(1, rows):
        total = total + dot_nt(dz[:, k * width : (k + 1) * width], out_s[k])
    datt_s[...] = total.astype(LOW)
    span = heads * HD
    two = 2 * HD
    scale = 1.0 / math.sqrt(HD)
    lane = lax.broadcasted_iota(jnp.int32, (1, two), 1)
    for pair in range(heads // 2):
        at = pair * two
        queries = packed[:, at : at + two]
        key_rows = packed[:, span + at : span + at + two]
        values = packed[:, 2 * span + at : 2 * span + at + two]
        grads = datt_s[:, at : at + two]
        dqs, dks, dvs = [], [], []
        for side in range(2):
            mask = (lane < HD) if side == 0 else (lane >= HD)
            probs = soft(dot_nt(jnp.where(mask, queries, jnp.zeros_like(queries)), key_rows))
            dprobs = dot_nt(jnp.where(mask, grads, jnp.zeros_like(grads)), values)
            dscores = probs * (dprobs - jnp.sum(dprobs * probs, axis=-1, keepdims=True))
            dscores = dscores.astype(LOW)
            dqs.append(dot_nn(dscores, key_rows))
            dks.append(dot_tn(dscores, queries))
            dvs.append(dot_tn(probs.astype(LOW), grads))
        first = lane < HD
        dpacked_o[:, at : at + two] = (jnp.where(first, dqs[0], dqs[1]) * scale).astype(LOW)
        dpacked_o[:, span + at : span + at + two] = (jnp.where(first, dks[0], dks[1]) * scale).astype(LOW)
        dpacked_o[:, 2 * span + at : 2 * span + at + two] = jnp.where(first, dvs[0], dvs[1]).astype(LOW)
    psum_o[...] = jnp.sum(dpacked_o[...].astype(WIDE), axis=0, keepdims=True)
    for k in range(rows):
        back_o[:, k * width : (k + 1) * width] = dot_nn(dpacked_o[...], qkv_s[k]).astype(LOW)


def attn_grad_kernel(spec, pos, *refs):
    n, rows, heads, width = spec
    dpacked, normed, att, dz = refs[0:2], refs[2:4], refs[4:6], refs[6:8]
    outs, total_s = refs[8 : 8 + n], refs[8 + n]
    me = pos[1]
    span = heads * HD
    own = HD // n
    for part in range(4):
        if part < 3:
            at = slice(part * span, (part + 1) * span)
            total = dot_tn(dpacked[0][:, at], normed[0][...]) + dot_tn(dpacked[1][:, at], normed[1][...])
        else:
            total = dot_tn(att[0][...], dz[0][...]) + dot_tn(att[1][...], dz[1][...])
        total_s[...] = total.astype(LOW)
        for d in range(n):
            place = me ^ d if n > 1 else 0
            for g in range(heads):
                line = g * HD + place * own
                if n > 1:
                    line = pl.multiple_of(line, own)
                value = total_s[pl.ds(line, own), :]
                to = (part * heads + g) * own
                for k in range(rows):
                    outs[d][k, to : to + own, :] = value[:, k * width : (k + 1) * width]


def last_kernel(spec, pos, vec, *refs):
    rows, width, images = spec
    x, back, came, dmid = (refs[i * images : (i + 1) * images] for i in range(4))
    out_o, sums_o = refs[4 * images :]
    low_col = pos[0] == 0
    half = width // 2
    for i in range(images):
        scaled, inv_std = moments_of(x[i][...].astype(WIDE))
        grad_norm = back[i][...].astype(WIDE) + came[i][...].astype(WIDE)
        value = dmid[i][...] + norm_backward(grad_norm, scaled, inv_std, vec[0:1, :])
        gain_sum = jnp.sum(grad_norm * scaled, axis=0, keepdims=True)
        shift_sum = jnp.sum(grad_norm, axis=0, keepdims=True)
        if i == 0:
            sums_o[0:1, :] = gain_sum
            sums_o[1:2, :] = shift_sum
        else:
            sums_o[0:1, :] += gain_sum
            sums_o[1:2, :] += shift_sum
        for k in range(rows):
            left, right = value[:, k * width : k * width + half], value[:, k * width + half : (k + 1) * width]
            out_o[k, i] = jnp.where(low_col, left, right).astype(LOW)


ROOM = 56 * 1024 * 1024


def whole(array):
    zeros = (0,) * len(array.shape)
    return pl.BlockSpec(tuple(array.shape), lambda *_: zeros)


def run_kernel(body, args, outs, scratch=(), grid=None, in_specs=None, out_specs=None, flops=0):
    if in_specs is None:
        in_specs = [pl.BlockSpec(memory_space=pltpu.SMEM)] + [whole(a) for a in args[1:]]
    if out_specs is None:
        out_specs = [whole(o) for o in outs]
    size = sum(math.prod(a.shape) * a.dtype.itemsize for a in (*args, *outs))
    return pl.pallas_call(
        body,
        grid=grid or (1,),
        in_specs=in_specs,
        out_specs=out_specs,
        out_shape=outs,
        scratch_shapes=list(scratch),
        compiler_params=pltpu.CompilerParams(vmem_limit_bytes=ROOM),
        cost_estimate=pl.CostEstimate(flops=flops, bytes_accessed=size, transcendentals=0),
    )(*args)


def shaped(shape, kind):
    return jax.ShapeDtypeStruct(shape, kind)


def on_device(
    tokens, cotangent, w_qkv, b_qkv, w_out, w_up, b_up, w_down, vectors,
    state_qkv, state_qkv_bias, state_out, state_up, state_up_bias, state_down, state_vectors,
):
    parts, rows = lax.axis_size("dp"), lax.axis_size("row")
    col, row_index, me = lax.axis_index("col"), lax.axis_index("row"), lax.axis_index("dp")
    low_col = col == 0
    width = w_qkv.shape[0]
    heads, chunk = w_qkv.shape[2], w_qkv.shape[3]
    groups = w_up.shape[1]
    strip = tokens.shape[1]
    images = tokens.shape[0] // (SEQ * rows)
    model = rows * width
    span = heads * HD
    units = groups * HD
    pos = jnp.stack([col, me]).astype(jnp.int32)

    qkv_own = w_qkv.transpose(1, 2, 3, 0).reshape(-1, width)
    out_own = w_out.reshape(-1, width)
    up_own = w_up.transpose(1, 2, 0).reshape(-1, width)
    down_own = w_down.reshape(-1, width)
    qkv_count, out_count, up_count = qkv_own.shape[0], out_own.shape[0], up_own.shape[0]

    at_me = (jnp.arange(parts) == me)[:, None]
    vec_own = jnp.where(at_me, vectors[:, :, None, :], 0).reshape(6, -1)
    vec_far = swap_col(vec_own)
    vec_pair = jnp.stack([jnp.where(low_col, vec_own, vec_far), jnp.where(low_col, vec_far, vec_own)])
    bias_own = jnp.where(at_me, b_qkv[:, :, None, :], 0).reshape(-1, width)
    blocks_up = up_count // out_count
    unit_own = jnp.where(at_me, b_up.reshape(blocks_up, 1, -1), 0).reshape(-1, width)
    small_count = 6 + bias_own.shape[0] + unit_own.shape[0]
    small_pad = -small_count % 16

    def to_images(stream, extra):
        blocks = stream.astype(LOW).reshape(rows, images, SEQ, strip)
        blocks = jnp.pad(blocks, ((0, 0), (0, 0), (0, PAD - SEQ), (0, 0)))
        if extra is not None:
            extra = jnp.pad(extra, ((0, 0), (0, 2), (0, 0)))
            blocks = jnp.concatenate([blocks, jnp.broadcast_to(extra, (rows, *extra.shape))], axis=2)
        came = [lax.dynamic_index_in_dim(blocks, row_index, 0, False)]
        for k in range(1, rows):
            came.append(turn(lax.dynamic_index_in_dim(blocks, (row_index + k) % rows, 0, False), k))
        near = jnp.stack([block[:, :PAD] for block in came])
        return near, swap_col(near), came

    first = gather_row(qkv_own)
    near, far, came = to_images(tokens, vec_pair)
    vec_rows = [jnp.concatenate([block[0, PAD : PAD + 6], block[1, PAD : PAD + 6]], axis=1) for block in came]
    tail_rows = [
        jnp.concatenate([block, bias_own, unit_own, jnp.zeros((small_pad, width), LOW)]) for block in vec_rows
    ]
    first = jnp.stack([jnp.concatenate([a, b]) for a, b in zip(first, tail_rows)])
    first_all = gather_dp(first)
    second_all = gather_dp(jnp.stack(gather_row(jnp.concatenate([out_own, up_own]))))
    third_all = gather_dp(jnp.stack(gather_row(down_own)))
    near_dy, far_dy, _ = to_images(cotangent, None)

    own = chunk
    if chunk % 16:
        own = HD

        def merge(blocks, lead):
            both = xor_order(jnp.stack(blocks), 0).reshape(parts, rows, lead, -1, width)
            return both.transpose(1, 2, 0, 3, 4).reshape(rows, -1, width)

        heads_rows = merge([b[:, :qkv_count] for b in first_all], 3 * heads)
        small_rows = sum(b[:, qkv_count:].astype(WIDE) for b in first_all).astype(LOW)
        first_all = [jnp.concatenate([heads_rows, small_rows], axis=1)]
        out_rows = merge([b[:, :out_count] for b in second_all], heads)
        up_rows = merge([b[:, out_count:] for b in second_all], blocks_up)
        second_all = [jnp.concatenate([out_rows, up_rows], axis=1)]
        third_all = [merge(third_all, blocks_up)]
    n = len(first_all)
    out_rows_each = out_count * parts // n

    def source_specs(blocks, count, moving=None):
        if moving is None:
            return [pl.BlockSpec((rows, count, width), lambda *_: (0, 0, 0)) for _ in blocks]
        return [pl.BlockSpec((rows, count, width), lambda u: (0, u + moving, 0)) for _ in blocks]

    scalars = pl.BlockSpec(memory_space=pltpu.SMEM)
    first_rows = first_all[0].shape[1]

    def forward_one(i):
        strips = pl.BlockSpec((rows, 1, PAD, strip), lambda *_: (0, i, 0, 0))
        outs = [
            shaped((8, model), WIDE),
            shaped((PAD, model), LOW),
            shaped((PAD, model), LOW),
            shaped((PAD, 3 * span), LOW),
            shaped((PAD, span), LOW),
            shaped((PAD, model), LOW),
        ]
        return run_kernel(
            functools.partial(first_kernel, (n, rows, heads, width)),
            (pos, near, far, *first_all, *second_all),
            outs,
            scratch=[pltpu.VMEM((rows, 3 * span, width), LOW), pltpu.VMEM((rows, span, width), LOW)],
            in_specs=[scalars, strips, strips, *source_specs(first_all, first_rows), *source_specs(second_all, out_rows_each)],
            flops=10**10,
        )

    done = [forward_one(i) for i in range(images)]
    vec = done[0][0]
    came_one = [swap_col(d[5]) for d in done]

    unit_rows = sum(b[0, qkv_count * parts // n + 6 + bias_own.shape[0] :][: unit_own.shape[0]].astype(WIDE) for b in first_all)
    unit_rows = unit_rows.reshape(blocks_up, parts, -1)
    if n > 1:
        unit_rows = xor_order(unit_rows, 1)
    unit_rows = unit_rows.reshape(blocks_up, 1, -1)
    block_units = units // blocks_up

    def feed_one(i):
        strips = pl.BlockSpec((rows, 1, PAD, strip), lambda *_: (0, i, 0, 0))
        x, part = done[i][1], done[i][5]
        outs = [
            shaped((PAD, model), WIDE),
            shaped((PAD, model), LOW),
            shaped((PAD, model), LOW),
            shaped((PAD, units), LOW),
            shaped((PAD, units), LOW),
            shaped((1, units), WIDE),
            shaped((1, model), WIDE),
            shaped((rows, PAD, strip), WIDE),
            shaped((rows, PAD, strip), LOW),
            shaped((PAD, model), LOW),
        ]
        by_block = lambda lead: pl.BlockSpec((lead, block_units), lambda u: (0, u))
        out_specs = [whole(o) for o in outs]
        out_specs[3], out_specs[4], out_specs[5] = by_block(PAD), by_block(PAD), by_block(1)
        return run_kernel(
            functools.partial(feed_kernel, (n, rows, groups, width, block_units)),
            (pos, vec, unit_rows, x, part, came_one[i], near_dy, far_dy, *second_all, *third_all),
            outs,
            scratch=[pltpu.VMEM((PAD, model), WIDE), pltpu.VMEM((PAD, model), WIDE)],
            grid=(blocks_up,),
            in_specs=[
                scalars, whole(vec), pl.BlockSpec((1, 1, block_units), lambda u: (u, 0, 0)), whole(x), whole(part), whole(part),
                strips, strips,
                *source_specs(second_all, out_rows_each, 1), *source_specs(third_all, out_rows_each, 0),
            ],
            out_specs=out_specs,
            flops=10**10,
        )

    fed = [feed_one(i) for i in range(images)]
    came_two = [swap_col(f[9]) for f in fed]

    def feed_grad(lefts, rights):
        each = out_rows_each
        outs = [shaped((rows, each * blocks_up, width), LOW) for _ in range(n)]
        return run_kernel(
            functools.partial(feed_grad_kernel, (n, rows, width)),
            (*lefts, *rights),
            outs,
            grid=(blocks_up,),
            in_specs=[pl.BlockSpec((PAD, block_units), lambda u: (0, u)) for _ in lefts] + [whole(r) for r in rights],
            out_specs=[pl.BlockSpec((rows, each, width), lambda u: (0, u, 0)) for _ in range(n)],
            flops=10**10,
        )

    def split_sources(blocks, lead):
        if n == parts:
            return blocks
        split = blocks[0].reshape(rows, lead, parts, -1, width).transpose(2, 0, 1, 3, 4)
        split = xor_order(split.reshape(parts, rows, -1, width), 0)
        return [split[d] for d in range(parts)]

    down_grad = feed_grad([f[3] for f in fed], [f[2] for f in fed])
    up_grad = feed_grad([f[4] for f in fed], [f[1] for f in fed])

    def reduce_all(blocks):
        held = scatter_dp(blocks, LOW)
        return scatter_row([held[k] for k in range(rows)])

    feed_down = reduce_all(split_sources(down_grad, blocks_up))
    feed_up = reduce_all(split_sources(up_grad, blocks_up))

    def from_images(strips):
        came = [strips[0]] + [turn(strips[k], -k) for k in range(1, rows)]
        stacked = jnp.stack(came)[:, :, :SEQ]
        order = (jnp.arange(rows) - row_index) % rows
        return stacked[order].reshape(-1, strip).astype(WIDE)

    top = jnp.stack([f[7] + swap_col(f[8]).astype(WIDE) for f in fed], axis=1).astype(LOW)
    result = from_images(top)

    def backward_one(i):
        outs = [
            shaped((PAD, model), WIDE),
            shaped((PAD, model), LOW),
            shaped((PAD, 3 * span), LOW),
            shaped((PAD, model), LOW),
            shaped((8, model), WIDE),
            shaped((1, 3 * span), WIDE),
        ]
        acts = (vec, fed[i][0], fed[i][9], came_two[i], fed[i][2], done[i][3])
        return run_kernel(
            functools.partial(second_kernel, (n, rows, heads, width)),
            (pos, *acts, *first_all, *second_all),
            outs,
            scratch=[
                pltpu.VMEM((rows, 3 * span, width), LOW), pltpu.VMEM((rows, span, width), LOW), pltpu.VMEM((PAD, span), LOW),
            ],
            in_specs=[
                scalars, *[whole(a) for a in acts], *source_specs(first_all, first_rows), *source_specs(second_all, out_rows_each),
            ],
            flops=10**10,
        )

    returned = [backward_one(i) for i in range(images)]
    came_three = [swap_col(r[3]) for r in returned]
    attn_grad = run_kernel(
        functools.partial(attn_grad_kernel, (n, rows, heads, width)),
        (
            pos, *[r[2] for r in returned], *[d[2] for d in done], *[d[4] for d in done], *[r[1] for r in returned],
        ),
        [shaped((rows, (qkv_count + out_count) * parts // n, width), LOW) for _ in range(n)],
        scratch=[pltpu.VMEM((span, model), LOW)],
        flops=10**10,
    )
    attn = reduce_all(split_sources(attn_grad, 4 * heads))
    grad_strips, sums_one = run_kernel(
        functools.partial(last_kernel, (rows, width, images)),
        (
            pos, vec, *[d[1] for d in done], *[r[3] for r in returned], *came_three, *[r[0] for r in returned],
        ),
        [shaped((rows, images, PAD, strip), LOW), shaped((8, model), WIDE)],
        flops=10**9,
    )
    grad_tokens = from_images(grad_strips)

    sums_two = sum(r[4] for r in returned)
    dy_sum = sum(f[6] for f in fed)
    vector_sum = jnp.concatenate([sums_one[0:2], sums_two[0:3], dy_sum])
    packed_sum = sum(r[5] for r in returned).reshape(3, heads, parts, chunk)
    packed_sum = xor_order(jnp.stack([packed_sum[0], packed_sum[2]]).transpose(2, 0, 1, 3), 0).reshape(parts, -1)
    unit_sum = sum(f[5] for f in fed).reshape(blocks_up, parts, -1).transpose(1, 0, 2)
    if n == 1:
        unit_sum = xor_order(unit_sum, 0)
    unit_sum = unit_sum.reshape(parts, -1)
    vector_split = vector_sum.reshape(6, rows, 2, 2, parts, chunk)
    vector_split = jnp.where(low_col, vector_split[:, :, 0], vector_split[:, :, 1])
    vector_split = xor_order(vector_split.transpose(3, 1, 0, 2, 4), 0)
    vector_split = vector_split[:, (row_index - jnp.arange(rows)) % rows]
    tiny = jnp.concatenate([packed_sum, unit_sum, vector_split.reshape(parts, -1)], axis=1)
    tiny = scatter_dp([tiny[d] for d in range(parts)], WIDE)
    tiny = lax.psum(tiny, "row")
    size_packed, size_unit = packed_sum.shape[1], unit_sum.shape[1]
    tiny_vec = tiny[size_packed + size_unit :].reshape(rows, 6, 2, chunk)
    tiny_vec = lax.dynamic_index_in_dim(tiny_vec, row_index, 0, False)

    attn_qkv, attn_out = attn[:qkv_count], attn[qkv_count:]
    summed = (
        attn_qkv.reshape(3, heads, chunk, width).transpose(3, 0, 1, 2),
        tiny[:size_packed].reshape(b_qkv.shape),
        attn_out.reshape(w_out.shape),
        feed_up.reshape(groups, chunk, width).transpose(2, 0, 1),
        tiny[size_packed : size_packed + size_unit].reshape(b_up.shape),
        feed_down.reshape(w_down.shape),
        tiny_vec,
    )
    grad_scale = grad_gain / math.sqrt(tokens.shape[0] * parts)
    old_params = (w_qkv, b_qkv, w_out, w_up, b_up, w_down, vectors)
    states = (state_qkv, state_qkv_bias, state_out, state_up, state_up_bias, state_down, state_vectors)
    decays = (weight_decay, 0.0, weight_decay, weight_decay, 0.0, weight_decay, 0.0)
    scaled, updated, fresh = [], [], []
    for number in range(7):
        gradient = summed[number] * grad_scale
        change, moments = adam_step(old_params[number].astype(WIDE), gradient, states[number], decays[number])
        scaled.append(gradient)
        updated.append(change)
        fresh.append(moments)
    return (result, grad_tokens, *scaled, *updated, *fresh)


def solution(mesh):
    placed = (
        P("dp", ("row", "col")),
        P("dp", ("row", "col")),
        P("row", None, "col", "dp"),
        P(None, "col", "dp"),
        P("col", "dp", "row"),
        P("row", "col", "dp"),
        P("col", "dp"),
        P("col", "dp", "row"),
        P(None, ("row", "col"), "dp"),
        P(None, "row", None, "col", "dp"),
        P(None, None, "col", "dp"),
        P(None, "col", "dp", "row"),
        P(None, "row", "col", "dp"),
        P(None, "col", "dp"),
        P(None, "col", "dp", "row"),
        P(None, None, ("row", "col"), "dp"),
    )
    params = placed[2:9]
    return jax.shard_map(
        on_device,
        mesh=mesh,
        in_specs=placed,
        out_specs=(placed[0], placed[0], *params, *params, *placed[9:]),
        check_vma=False,
    )
```

time: 578 us -> 394 us (0.68)
  the two profiles are of different devices: /device:TPU:0 before, /device:TPU:9 now
where the time goes in v2:
time: 394 us; the launch traced here: 389 us
  waiting for transfers between devices  126 us (32%)
  starting transfers between devices  97.4 us (25%)
  Pallas kernels  77.4 us (20%)
  other arithmetic  40.7 us (10%)
  local copies, waits for them, and re-layouts  38.2 us (10%)
  blocking collectives  7.56 us (2%)
    pallas_call x10, Pallas kernels, run_kernel(): pl.pallas_call(body, grid=grid or (1,), in_specs=in_specs, out_specs=out_...  77.4 us
    ppermute x30, waiting for transfers between devices, turn(): lax.ppermute(values, 'row', [(i, (i + shift) % count) for i in range(coun...  76 us
    ppermute x30, starting transfers between devices, turn(): lax.ppermute(values, 'row', [(i, (i + shift) % count) for i in range(coun...  44.4 us
    ppermute x21, starting transfers between devices, swap_dp(): return lax.ppermute(values, 'dp', [(i, i ^ bit) for i in range(count)])  44.1 us
    ppermute x11, waiting for transfers between devices, swap_col(): return lax.ppermute(values, 'col', [(0, 1), (1, 0)])  30 us
    ppermute x21, waiting for transfers between devices, swap_dp(): return lax.ppermute(values, 'dp', [(i, i ^ bit) for i in range(count)])  20.4 us
    unnamed x120, local copies, waits for them, and re-layouts  10.3 us
    ppermute x11, starting transfers between devices, swap_col(): return lax.ppermute(values, 'col', [(0, 1), (1, 0)])  8.91 us
  transfers between devices with their start and end apart: 62, of which 17 were waited for; matrix products, arithmetic and copies ran while one was open for 17% of the time, Pallas kernels for 20%

profile of v2, /device:TPU:9, one launch (start us, length us, event | category | flops | bytes accessed | tf_op | source)
XLA Modules:
  0.0 389.4 jit_solution(11951292950994825711)
XLA Ops:
  1.8 2.5 collective-permute-start.12
  4.3 2.2 collective-permute-start.11
  12.5 2.1 collective-permute-start.3
  15.0 23.0 %collective-permute-done.3 = bf16[2,216,128]{2,1,0:T(8,128)(2,1)S(1)} collective-permute-done((bf16[2,216,128]{2,1,0:T(8,128)(2,1)S(1)}, bf16[2,216,128]{2,1,0:T(8,128)(2,1)S(1)}, u32[]{:S(2)}, u32[]{:S(2)}) %collective-permute-start.3) | collective-permute-done | bytes 110624 | tf_op jit(solution)/shard_map/ppermute | solution.py:30
  38.1 5.3 %collective-permute-done.2 = bf16[2,216,128]{2,1,0:T(8,128)(2,1)S(1)} collective-permute-done((bf16[2,216,128]{2,1,0:T(8,128)(2,1)S(1)}, bf16[2,216,128]{2,1,0:T(8,128)(2,1)S(1)}, u32[]{:S(2)}, u32[]{:S(2)}) %collective-permute-start.2) | collective-permute-done | bytes 110624 | tf_op jit(solution)/shard_map/ppermute | solution.py:30
  43.4 3.6 collective-permute-done.1
  47.0 3.1 collective-permute-start.6
  56.3 2.0 collective-permute-done.6
  58.2 7.2 %collective-permute-start.18 = (bf16[2,208,128]{2,1,0:T(8,128)(2,1)}, bf16[2,208,128]{2,1,0:T(8,128)(2,1)}, u32[]{:S(2)}, u32[]{:S(2)}) collective-permute-start(bf16[2,208,128]{2,1,0:T(8,128)(2,1)} %get-tuple-element.237), channel_id=1, source_target_pairs={{0,2},{2,4},{4,6},{6,0},{1,3},{3,5},{5,7},{7,1},{8,10},{10,12},{12... | collective-permute-start | bytes 319496 | tf_op jit(solution)/shard_map/ppermute | solution.py:30
  71.8 1.9 collective-permute-start.24
  73.7 2.1 collective-permute-start.23
  75.8 2.5 collective-permute-start.22
  79.4 15.7 %collective-permute-start.8 = (bf16[4,416,256]{2,1,0:T(8,128)(2,1)}, bf16[4,416,256]{2,1,0:T(8,128)(2,1)S(1)}, u32[]{:S(2)}, u32[]{:S(2)}) collective-permute-start(bf16[4,416,256]{2,1,0:T(8,128)(2,1)} %pad_maximum_fusion.4.refs_0_), channel_id=1, source_target_pairs={{0,8},{8,0},{16,24},{24,16},{1,9},{9,1},{17,25},{25,17},{2,10},{10... | collective-permute-start | bytes 2555912 | tf_op jit(solution)/shard_map/ppermute | solution.py:39
  95.1 2.9 collective-permute-done.9.refs_2_
  98.0 4.5 %collective-permute-start.10 = (bf16[4,416,256]{2,1,0:T(8,128)(2,1)}, bf16[4,416,256]{2,1,0:T(8,128)(2,1)S(1)}, u32[]{:S(2)}, u32[]{:S(2)}) collective-permute-start(bf16[4,416,256]{2,1,0:T(8,128)(2,1)} %collective-permute-done.9.refs_2_), channel_id=1, source_target_pairs={{0,8},{8,0},{16,24},{24,16},{1,9},{9,1},{17,25},{25,17},{2,10},{10... | collective-permute-start | bytes 2555912 | tf_op jit(solution)/shard_map/ppermute | solution.py:39
  109.0 16.8 %collective-permute-done.4.far = bf16[4,2,208,128]{3,2,1,0:T(8,128)(2,1)} collective-permute-done((bf16[4,2,208,128]{3,2,1,0:T(8,128)(2,1)}, bf16[4,2,208,128]{3,2,1,0:T(8,128)(2,1)}, u32[]{:S(2)}, u32[]{:S(2)}) %collective-permute-start.4) | collective-permute-done | bytes 426016 | tf_op jit(solution)/shard_map/ppermute | solution.py:34
  129.1 6.2 %shard_map.335 = (f32[8,1024]{1,0:T(8,128)}, bf16[208,1024]{1,0:T(8,128)(2,1)}, bf16[208,1024]{1,0:T(8,128)(2,1)}, bf16[208,1536]{1,0:T(8,128)(2,1)}, bf16[208,5...) custom-call(s32[2]{0:T(128)} %pad_add_fusion.pos, bf16[4,2,208,128]{3,2,1,0:T(8,128)(2,1)} %pad_maximum_fusion.6.near, ...), custom_call_target="tpu_custom_call" | custom-call | flops 10000000000 | bytes 11665416 | tf_op jit(solution)/shard_map/pallas_call | solution.py:391
  136.5 6.2 %shard_map.337 = (f32[8,1024]{1,0:T(8,128)}, bf16[208,1024]{1,0:T(8,128)(2,1)}, bf16[208,1024]{1,0:T(8,128)(2,1)}, bf16[208,1536]{1,0:T(8,128)(2,1)}, bf16[208,5...) custom-call(s32[2]{0:T(128)} %pad_add_fusion.pos, bf16[4,2,208,128]{3,2,1,0:T(8,128)(2,1)} %pad_maximum_fusion.6.near, ...), custom_call_target="tpu_custom_call" | custom-call | flops 10000000000 | bytes 11665416 | tf_op jit(solution)/shard_map/pallas_call | solution.py:391
  143.0 4.0 %collective-permute-done.17.came = bf16[208,1024]{1,0:T(8,128)(2,1)S(1)} collective-permute-done((bf16[208,1024]{1,0:T(8,128)(2,1)}, bf16[208,1024]{1,0:T(8,128)(2,1)S(1)}, u32[]{:S(2)}, u32[]{:S(2)}) %collective-permute-start.17) | collective-permute-done | bytes 426016 | tf_op jit(solution)/shard_map/ppermute | solution.py:34
  147.7 10.6 %shard_map.336 = (f32[208,1024]{1,0:T(8,128)}, bf16[208,1024]{1,0:T(8,128)(2,1)}, bf16[208,1024]{1,0:T(8,128)(2,1)}, bf16[208,2048]{1,0:T(8,128)(2,1)}, bf16[208...) custom-call(s32[2]{0:T(128)} %pad_add_fusion.pos, ...), custom_call_target="tpu_custom_call" | custom-call | flops 10000000000 | bytes 16093192 | tf_op jit(solution)/shard_map/pallas_call | solution.py:391
  160.3 10.5 %shard_map.338 = (f32[208,1024]{1,0:T(8,128)}, bf16[208,1024]{1,0:T(8,128)(2,1)}, bf16[208,1024]{1,0:T(8,128)(2,1)}, bf16[208,2048]{1,0:T(8,128)(2,1)}, bf16[208...) custom-call(s32[2]{0:T(128)} %pad_add_fusion.pos, ...), custom_call_target="tpu_custom_call" | custom-call | flops 10000000000 | bytes 16093192 | tf_op jit(solution)/shard_map/pallas_call | solution.py:391
  172.6 6.2 %shard_map.343 = (bf16[4,512,256]{2,1,0:T(8,128)(2,1)}, bf16[4,512,256]{2,1,0:T(8,128)(2,1)}, bf16[4,512,256]{2,1,0:T(8,128)(2,1)}, bf16[4,512,256]{2,1,0:T(8,128)(2,1)}) custom-call(bf16[208,2048]{1,0:T(8,128)(2,1)} %get-tuple-element.123.refs_0_, bf16[208,2048]{1,0:T(8,128)(2,1)} %get-tuple-element.124.refs_1_, ...), custom_call_target="tpu_custom_call" | custom-call | flops 10000000000 | bytes 6750208 | tf_op jit(solution)/shard_map/pallas_call | solution.py:391
  180.0 2.8 collective-permute-start.32
  182.8 6.5 %shard_map.344 = (bf16[4,512,256]{2,1,0:T(8,128)(2,1)}, bf16[4,512,256]{2,1,0:T(8,128)(2,1)}, bf16[4,512,256]{2,1,0:T(8,128)(2,1)}, bf16[4,512,256]{2,1,0:T(8,128)(2,1)}) custom-call(bf16[208,2048]{1,0:T(8,128)(2,1)} %get-tuple-element.131.refs_0_, bf16[208,2048]{1,0:T(8,128)(2,1)} %get-tuple-element.132.refs_1_, ...), custom_call_target="tpu_custom_call" | custom-call | flops 10000000000 | bytes 6750208 | tf_op jit(solution)/shard_map/pallas_call | solution.py:391
  189.4 2.9 collective-permute-start.51
  194.6 10.1 %shard_map.339 = (f32[208,1024]{1,0:T(8,128)}, bf16[208,1024]{1,0:T(8,128)(2,1)}, bf16[208,1536]{1,0:T(8,128)(2,1)}, bf16[208,1024]{1,0:T(8,128)(2,1)}, f32[8,1024]{1,0:T(8,128)}, /*index=5*/f32[1,1536]{1,0:T(1,128)}) custom-call(s32[2]{0:T(128)} %pad_add_fusion.pos, f32[8,1024]{1,0:T(8,128)} %get-tuple-element.80.vec, f32[208,1024]{1,0:T(8,128)} %get-tuple-element.89.mid, ...), custom_call_target="tpu_custom_call" | custom-call | flops 10000000000 | bytes 13834248 | tf_op jit(solution)/shard_map/pallas_call | solution.py:391
  206.0 10.2 %shard_map.340 = (f32[208,1024]{1,0:T(8,128)}, bf16[208,1024]{1,0:T(8,128)(2,1)}, bf16[208,1536]{1,0:T(8,128)(2,1)}, bf16[208,1024]{1,0:T(8,128)(2,1)}, f32[8,1024]{1,0:T(8,128)}, /*index=5*/f32[1,1536]{1,0:T(1,128)}) custom-call(s32[2]{0:T(128)} %pad_add_fusion.pos, f32[8,1024]{1,0:T(8,128)} %get-tuple-element.80.vec, f32[208,1024]{1,0:T(8,128)} %get-tuple-element.94.mid, ...), custom_call_target="tpu_custom_call" | custom-call | flops 10000000000 | bytes 13834248 | tf_op jit(solution)/shard_map/pallas_call | solution.py:391
  218.2 9.2 %collective-permute-done.37.refs_5_ = bf16[208,1024]{1,0:T(8,128)(2,1)S(1)} collective-permute-done((bf16[208,1024]{1,0:T(8,128)(2,1)}, bf16[208,1024]{1,0:T(8,128)(2,1)S(1)}, u32[]{:S(2)}, u32[]{:S(2)}) %collective-permute-start.37) | collective-permute-done | bytes 426016 | tf_op jit(solution)/shard_map/ppermute | solution.py:34
  228.1 4.6 %shard_map.341 = (bf16[4,2,208,128]{3,2,1,0:T(8,128)(2,1)}, f32[8,1024]{1,0:T(8,128)}) custom-call(s32[2]{0:T(128)} %pad_add_fusion.pos, f32[8,1024]{1,0:T(8,128)} %get-tuple-element.80.vec, bf16[208,1024]{1,0:T(8,128)(2,1)} %get-tuple-element.81.x.refs_0_, bf16[208,1024]{1,0:T(8,128)(2,1)} %get-tuple-element.85.x.refs_1_, ...), custom_call_target="tpu_custom_call" | custom-call | flops 1000000000 | bytes 4751368 | tf_op jit(solution)/shard_map/pallas_call | solution.py:391
  236.4 6.4 %shard_map.342 = (bf16[4,512,256]{2,1,0:T(8,128)(2,1)}, bf16[4,512,256]{2,1,0:T(8,128)(2,1)}, bf16[4,512,256]{2,1,0:T(8,128)(2,1)}, bf16[4,512,256]{2,1,0:T(8,128)(2,1)}) custom-call(s32[2]{0:T(128)} %pad_add_fusion.pos, bf16[208,1536]{1,0:T(8,128)(2,1)} %get-tuple-element.102.refs_0_, bf16[208,1536]{1,0:T(8,128)(2,1)} %get-tuple-element.103.refs_1_, ...), custom_call_target="tpu_custom_call" | custom-call | flops 10000000000 | bytes 7602184 | tf_op jit(solution)/shard_map/pallas_call | solution.py:391
  245.6 1.7 collective-permute-start.40
  248.0 7.6 %psum.7 = f32[1536]{0:T(1024)} all-reduce(f32[1536]{0:T(1024)} %add_add_fusion), channel_id=1, replica_groups=mesh['dp'=4,'row'=4,'col'=2] {'row'}, use_global_device_ids=true, to_apply=%region_0.1 | all-reduce | flops 1536 | bytes 12288 | tf_op jit(solution)/shard_map/psum | solution.py:655
  285.5 1.5 collective-permute-start.38
  287.3 1.5 collective-permute-done.39
  288.8 4.8 %collective-permute-start.56 = (bf16[4,512,256]{2,1,0:T(8,128)(2,1)}, bf16[4,512,256]{2,1,0:T(8,128)(2,1)}, u32[]{:S(2)}, u32[]{:S(2)}) collective-permute-start(bf16[4,512,256]{2,1,0:T(8,128)(2,1)} %get-tuple-element.134), channel_id=1, source_target_pairs={{0,8},{8,0},{16,24},{24,16},{1,9},{9,1},{17,25},{25,17},{2,10},{10... | collective-permute-start | bytes 3145736 | tf_op jit(solution)/shard_map/ppermute | solution.py:39
  299.2 3.4 collective-permute-start.41
  302.6 1.6 add_convert_fusion.7
  305.5 2.0 add_convert_fusion.3
  308.1 2.5 collective-permute-start.54
  310.6 16.2 %collective-permute-done.58 = bf16[4,512,256]{2,1,0:T(8,128)(2,1)} collective-permute-done((bf16[4,512,256]{2,1,0:T(8,128)(2,1)S(1)}, bf16[4,512,256]{2,1,0:T(8,128)(2,1)}, u32[]{:S(2)}, u32[]{:S(2)}) %collective-permute-start.58) | collective-permute-done | bytes 1048608 | tf_op jit(solution)/shard_map/ppermute | solution.py:39
  326.8 2.1 collective-permute-start.53
  328.9 2.0 add_convert_fusion
  331.1 2.1 collective-permute-start.60
  337.0 16.7 %collective-permute-done.60 = bf16[512,256]{1,0:T(8,128)(2,1)S(1)} collective-permute-done((bf16[512,256]{1,0:T(8,128)(2,1)S(1)}, bf16[512,256]{1,0:T(8,128)(2,1)S(1)}, u32[]{:S(2)}, u32[]{:S(2)}) %collective-permute-start.60) | collective-permute-done | bytes 262176 | tf_op jit(solution)/shard_map/ppermute | solution.py:30
  353.7 2.8 collective-permute-done.59
  363.1 2.6 collective-permute-done.46
  365.7 13.8 %collective-permute-done.45 = bf16[512,256]{1,0:T(8,128)(2,1)S(1)} collective-permute-done((bf16[512,256]{1,0:T(8,128)(2,1)S(1)}, bf16[512,256]{1,0:T(8,128)(2,1)S(1)}, u32[]{:S(2)}, u32[]{:S(2)}) %collective-permute-start.45) | collective-permute-done | bytes 262176 | tf_op jit(solution)/shard_map/ppermute | solution.py:30
  379.5 4.6 %collective-permute-done.44 = bf16[512,256]{1,0:T(8,128)(2,1)S(1)} collective-permute-done((bf16[512,256]{1,0:T(8,128)(2,1)S(1)}, bf16[512,256]{1,0:T(8,128)(2,1)S(1)}, u32[]{:S(2)}, u32[]{:S(2)}) %collective-permute-start.44) | collective-permute-done | bytes 262176 | tf_op jit(solution)/shard_map/ppermute | solution.py:30
  (347 shorter events, 104.6 us)
Async XLA Ops:
  1.8 48.3 %collective-permute-start.13 = (bf16[640,256]{1,0:T(8,128)(2,1)S(1)}, bf16[640,256]{1,0:T(8,128)(2,1)}, u32[]{:S(2)}, u32[]{:S(2)}) collective-permute-start(bf16[640,256]{1,0:T(8,128)(2,1)S(1)} %get-tuple-element.241), channel_id=1, source_target_pairs={{0,6},{2,0},{4,2},{6,4},{1,7},{3,1},{5,3},{7,5},{8,14},{10,8},{12,... | collective-permute-start | bytes 983048 | tf_op jit(solution)/shard_map/ppermute | solution.py:30
  1.8 49.2 %collective-permute-start.12 = (bf16[640,256]{1,0:T(8,128)(2,1)S(1)}, bf16[640,256]{1,0:T(8,128)(2,1)}, u32[]{:S(2)}, u32[]{:S(2)}) collective-permute-start(bf16[640,256]{1,0:T(8,128)(2,1)S(1)} %get-tuple-element.241), channel_id=1, source_target_pairs={{0,4},{2,6},{4,0},{6,2},{1,5},{3,7},{5,1},{7,3},{8,12},{10,14},{12... | collective-permute-start | bytes 983048 | tf_op jit(solution)/shard_map/ppermute | solution.py:30
  4.3 47.3 %collective-permute-start.11 = (bf16[640,256]{1,0:T(8,128)(2,1)S(1)}, bf16[640,256]{1,0:T(8,128)(2,1)}, u32[]{:S(2)}, u32[]{:S(2)}) collective-permute-start(bf16[640,256]{1,0:T(8,128)(2,1)S(1)} %get-tuple-element.241), channel_id=1, source_target_pairs={{0,2},{2,4},{4,6},{6,0},{1,3},{3,5},{5,7},{7,1},{8,10},{10,12},{12... | collective-permute-start | bytes 983048 | tf_op jit(solution)/shard_map/ppermute | solution.py:30
  8.7 45.5 %collective-permute-start.7 = (bf16[384,256]{1,0:T(8,128)(2,1)}, bf16[384,256]{1,0:T(8,128)(2,1)}, u32[]{:S(2)}, u32[]{:S(2)}) collective-permute-start(bf16[384,256]{1,0:T(8,128)(2,1)} %bitcast.357), channel_id=1, source_target_pairs={{0,6},{2,0},{4,2},{6,4},{1,7},{3,1},{5,3},{7,5},{8,14},{10,8},{12,... | collective-permute-start | bytes 589832 | tf_op jit(solution)/shard_map/ppermute | solution.py:30
  12.5 25.6 %collective-permute-start.3 = (bf16[2,216,128]{2,1,0:T(8,128)(2,1)S(1)}, bf16[2,216,128]{2,1,0:T(8,128)(2,1)S(1)}, u32[]{:S(2)}, u32[]{:S(2)}) collective-permute-start(bf16[2,216,128]{2,1,0:T(8,128)(2,1)S(1)} %get-tuple-element.225), channel_id=1, source_target_pairs={{0,6},{2,0},{4,2},{6,4},{1,7},{3,1},{5,3},{7,5},{8,14},{10,8},{12,... | collective-permute-start | bytes 331784 | tf_op jit(solution)/shard_map/ppermute | solution.py:30
  47.0 11.2 %collective-permute-start.6 = (bf16[384,256]{1,0:T(8,128)(2,1)S(1)}, bf16[384,256]{1,0:T(8,128)(2,1)S(1)}, u32[]{:S(2)}, u32[]{:S(2)}) collective-permute-start(bf16[384,256]{1,0:T(8,128)(2,1)S(1)} %bitcast.359), channel_id=1, source_target_pairs={{0,4},{2,6},{4,0},{6,2},{1,5},{3,7},{5,1},{7,3},{8,12},{10,14},{12... | collective-permute-start | bytes 589832 | tf_op jit(solution)/shard_map/ppermute | solution.py:30
  50.1 15.9 %collective-permute-start.5 = (bf16[384,256]{1,0:T(8,128)(2,1)S(1)}, bf16[384,256]{1,0:T(8,128)(2,1)S(1)}, u32[]{:S(2)}, u32[]{:S(2)}) collective-permute-start(bf16[384,256]{1,0:T(8,128)(2,1)S(1)} %bitcast.360), channel_id=1, source_target_pairs={{0,2},{2,4},{4,6},{6,0},{1,3},{3,5},{5,7},{7,1},{8,10},{10,12},{12... | collective-permute-start | bytes 589832 | tf_op jit(solution)/shard_map/ppermute | solution.py:30
  51.0 20.8 %collective-permute-start.20 = (bf16[2,208,128]{2,1,0:T(8,128)(2,1)}, bf16[2,208,128]{2,1,0:T(8,128)(2,1)}, u32[]{:S(2)}, u32[]{:S(2)}) collective-permute-start(bf16[2,208,128]{2,1,0:T(8,128)(2,1)} %get-tuple-element.239), channel_id=1, source_target_pairs={{0,6},{2,0},{4,2},{6,4},{1,7},{3,1},{5,3},{7,5},{8,14},{10,8},{12,... | collective-permute-start | bytes 319496 | tf_op jit(solution)/shard_map/ppermute | solution.py:30
  52.9 49.7 %collective-permute-start.15 = (bf16[4,640,256]{2,1,0:T(8,128)(2,1)S(1)}, bf16[4,640,256]{2,1,0:T(8,128)(2,1)}, u32[]{:S(2)}, u32[]{:S(2)}) collective-permute-start(bf16[4,640,256]{2,1,0:T(8,128)(2,1)S(1)} %pad_maximum_fusion.refs_4_.refs_0_), channel_id=1, source_target_pairs={{0,16},{8,24},{16,0},{24,8},{1,17},{9,25},{17,1},{25,9},{2,18},{10... | collective-permute-start | bytes 3932168 | tf_op jit(solution)/shard_map/ppermute | solution.py:39
  54.2 19.5 %collective-permute-start.19 = (bf16[2,208,128]{2,1,0:T(8,128)(2,1)}, bf16[2,208,128]{2,1,0:T(8,128)(2,1)S(1)}, u32[]{:S(2)}, u32[]{:S(2)}) collective-permute-start(bf16[2,208,128]{2,1,0:T(8,128)(2,1)} %get-tuple-element.238), channel_id=1, source_target_pairs={{0,4},{2,6},{4,0},{6,2},{1,5},{3,7},{5,1},{7,3},{8,12},{10,14},{12... | collective-permute-start | bytes 319496 | tf_op jit(solution)/shard_map/ppermute | solution.py:30
  58.2 17.6 %collective-permute-start.18 = (bf16[2,208,128]{2,1,0:T(8,128)(2,1)}, bf16[2,208,128]{2,1,0:T(8,128)(2,1)}, u32[]{:S(2)}, u32[]{:S(2)}) collective-permute-start(bf16[2,208,128]{2,1,0:T(8,128)(2,1)} %get-tuple-element.237), channel_id=1, source_target_pairs={{0,2},{2,4},{4,6},{6,0},{1,3},{3,5},{5,7},{7,1},{8,10},{10,12},{12... | collective-permute-start | bytes 319496 | tf_op jit(solution)/shard_map/ppermute | solution.py:30
  67.4 30.6 %collective-permute-start.9 = (bf16[4,416,256]{2,1,0:T(8,128)(2,1)}, bf16[4,416,256]{2,1,0:T(8,128)(2,1)}, u32[]{:S(2)}, u32[]{:S(2)}) collective-permute-start(bf16[4,416,256]{2,1,0:T(8,128)(2,1)} %pad_maximum_fusion.4.refs_0_), channel_id=1, source_target_pairs={{0,16},{8,24},{16,0},{24,8},{1,17},{9,25},{17,1},{25,9},{2,18},{10... | collective-permute-start | bytes 2555912 | tf_op jit(solution)/shard_map/ppermute | solution.py:39
  73.7 28.9 %collective-permute-start.23 = (bf16[512,256]{1,0:T(8,128)(2,1)S(1)}, bf16[512,256]{1,0:T(8,128)(2,1)S(1)}, u32[]{:S(2)}, u32[]{:S(2)}) collective-permute-start(bf16[512,256]{1,0:T(8,128)(2,1)S(1)} %bitcast.347), channel_id=1, source_target_pairs={{0,4},{2,6},{4,0},{6,2},{1,5},{3,7},{5,1},{7,3},{8,12},{10,14},{12... | collective-permute-start | bytes 786440 | tf_op jit(solution)/shard_map/ppermute | solution.py:30
  75.8 27.3 %collective-permute-start.22 = (bf16[512,256]{1,0:T(8,128)(2,1)S(1)}, bf16[512,256]{1,0:T(8,128)(2,1)S(1)}, u32[]{:S(2)}, u32[]{:S(2)}) collective-permute-start(bf16[512,256]{1,0:T(8,128)(2,1)S(1)} %bitcast.348), channel_id=1, source_target_pairs={{0,2},{2,4},{4,6},{6,0},{1,3},{3,5},{5,7},{7,1},{8,10},{10,12},{12... | collective-permute-start | bytes 786440 | tf_op jit(solution)/shard_map/ppermute | solution.py:30
  79.4 26.1 %collective-permute-start.8 = (bf16[4,416,256]{2,1,0:T(8,128)(2,1)}, bf16[4,416,256]{2,1,0:T(8,128)(2,1)S(1)}, u32[]{:S(2)}, u32[]{:S(2)}) collective-permute-start(bf16[4,416,256]{2,1,0:T(8,128)(2,1)} %pad_maximum_fusion.4.refs_0_), channel_id=1, source_target_pairs={{0,8},{8,0},{16,24},{24,16},{1,9},{9,1},{17,25},{25,17},{2,10},{10... | collective-permute-start | bytes 2555912 | tf_op jit(solution)/shard_map/ppermute | solution.py:39
  102.6 26.5 %collective-permute-start.14 = (bf16[4,640,256]{2,1,0:T(8,128)(2,1)S(1)}, bf16[4,640,256]{2,1,0:T(8,128)(2,1)}, u32[]{:S(2)}, u32[]{:S(2)}) collective-permute-start(bf16[4,640,256]{2,1,0:T(8,128)(2,1)S(1)} %pad_maximum_fusion.refs_4_.refs_0_), channel_id=1, source_target_pairs={{0,8},{8,0},{16,24},{24,16},{1,9},{9,1},{17,25},{25,17},{2,10},{10... | collective-permute-start | bytes 3932168 | tf_op jit(solution)/shard_map/ppermute | solution.py:39
  102.7 26.4 %collective-permute-start.16 = (bf16[4,640,256]{2,1,0:T(8,128)(2,1)}, bf16[4,640,256]{2,1,0:T(8,128)(2,1)}, u32[]{:S(2)}, u32[]{:S(2)}) collective-permute-start(bf16[4,640,256]{2,1,0:T(8,128)(2,1)} %collective-permute-done.15.refs_6_.refs_2_), channel_id=1, source_target_pairs={{0,8},{8,0},{16,24},{24,16},{1,9},{9,1},{17,25},{25,17},{2,10},{10... | collective-permute-start | bytes 3932168 | tf_op jit(solution)/shard_map/ppermute | solution.py:39
  103.3 24.9 %collective-permute-start.26 = (bf16[4,512,256]{2,1,0:T(8,128)(2,1)S(1)}, bf16[4,512,256]{2,1,0:T(8,128)(2,1)}, u32[]{:S(2)}, u32[]{:S(2)}) collective-permute-start(bf16[4,512,256]{2,1,0:T(8,128)(2,1)S(1)} %pad_maximum_fusion.1.refs_4_), channel_id=1, source_target_pairs={{0,16},{8,24},{16,0},{24,8},{1,17},{9,25},{17,1},{25,9},{2,18},{10... | collective-permute-start | bytes 3145736 | tf_op jit(solution)/shard_map/ppermute | solution.py:39
  105.5 37.5 %collective-permute-start.21 = (bf16[4,2,208,128]{3,2,1,0:T(8,128)(2,1)S(1)}, bf16[4,2,208,128]{3,2,1,0:T(8,128)(2,1)}, u32[]{:S(2)}, u32[]{:S(2)}) collective-permute-start(bf16[4,2,208,128]{3,2,1,0:T(8,128)(2,1)S(1)} %pad_maximum_fusion.7.near), channel_id=1, source_target_pairs={{0,1},{1,0},{2,3},{3,2},{4,5},{5,4},{6,7},{7,6},{8,9},{9,8},{10,11... | collective-permute-start | bytes 1277960 | tf_op jit(solution)/shard_map/ppermute | solution.py:34
  106.8 19.0 %collective-permute-start.4 = (bf16[4,2,208,128]{3,2,1,0:T(8,128)(2,1)}, bf16[4,2,208,128]{3,2,1,0:T(8,128)(2,1)}, u32[]{:S(2)}, u32[]{:S(2)}) collective-permute-start(bf16[4,2,208,128]{3,2,1,0:T(8,128)(2,1)} %pad_maximum_fusion.6.near), channel_id=1, source_target_pairs={{0,1},{1,0},{2,3},{3,2},{4,5},{5,4},{6,7},{7,6},{8,9},{9,8},{10,11... | collective-permute-start | bytes 1277960 | tf_op jit(solution)/shard_map/ppermute | solution.py:34
  125.8 17.1 %collective-permute-start.25 = (bf16[4,512,256]{2,1,0:T(8,128)(2,1)S(1)}, bf16[4,512,256]{2,1,0:T(8,128)(2,1)S(1)}, u32[]{:S(2)}, u32[]{:S(2)}) collective-permute-start(bf16[4,512,256]{2,1,0:T(8,128)(2,1)S(1)} %pad_maximum_fusion.1.refs_4_), channel_id=1, source_target_pairs={{0,8},{8,0},{16,24},{24,16},{1,9},{9,1},{17,25},{25,17},{2,10},{10... | collective-permute-start | bytes 3145736 | tf_op jit(solution)/shard_map/ppermute | solution.py:39
  128.2 14.8 %collective-permute-start.27 = (bf16[4,512,256]{2,1,0:T(8,128)(2,1)}, bf16[4,512,256]{2,1,0:T(8,128)(2,1)S(1)}, u32[]{:S(2)}, u32[]{:S(2)}) collective-permute-start(bf16[4,512,256]{2,1,0:T(8,128)(2,1)} %collective-permute-done.26.refs_6_), channel_id=1, source_target_pairs={{0,8},{8,0},{16,24},{24,16},{1,9},{9,1},{17,25},{25,17},{2,10},{10... | collective-permute-start | bytes 3145736 | tf_op jit(solution)/shard_map/ppermute | solution.py:39
  135.2 11.7 %collective-permute-start.17 = (bf16[208,1024]{1,0:T(8,128)(2,1)}, bf16[208,1024]{1,0:T(8,128)(2,1)S(1)}, u32[]{:S(2)}, u32[]{:S(2)}) collective-permute-start(bf16[208,1024]{1,0:T(8,128)(2,1)} %get-tuple-element.82.part), channel_id=1, source_target_pairs={{0,1},{1,0},{2,3},{3,2},{4,5},{5,4},{6,7},{7,6},{8,9},{9,8},{10,11... | collective-permute-start | bytes 1277960 | tf_op jit(solution)/shard_map/ppermute | solution.py:34
  142.7 16.9 %collective-permute-start.29 = (bf16[208,1024]{1,0:T(8,128)(2,1)}, bf16[208,1024]{1,0:T(8,128)(2,1)S(1)}, u32[]{:S(2)}, u32[]{:S(2)}) collective-permute-start(bf16[208,1024]{1,0:T(8,128)(2,1)} %get-tuple-element.86.part), channel_id=1, source_target_pairs={{0,1},{1,0},{2,3},{3,2},{4,5},{5,4},{6,7},{7,6},{8,9},{9,8},{10,11... | collective-permute-start | bytes 1277960 | tf_op jit(solution)/shard_map/ppermute | solution.py:34
  158.3 20.6 %collective-permute-start.28 = (bf16[4,208,128]{2,1,0:T(8,128)(2,1)}, bf16[4,208,128]{2,1,0:T(8,128)(2,1)S(1)}, u32[]{:S(2)}, u32[]{:S(2)}) collective-permute-start(bf16[4,208,128]{2,1,0:T(8,128)(2,1)} %get-tuple-element.84), channel_id=1, source_target_pairs={{0,1},{1,0},{2,3},{3,2},{4,5},{5,4},{6,7},{7,6},{8,9},{9,8},{10,11... | collective-permute-start | bytes 638984 | tf_op jit(solution)/shard_map/ppermute | solution.py:34
  171.2 23.4 %collective-permute-start.34 = (bf16[208,1024]{1,0:T(8,128)(2,1)}, bf16[208,1024]{1,0:T(8,128)(2,1)}, u32[]{:S(2)}, u32[]{:S(2)}) collective-permute-start(bf16[208,1024]{1,0:T(8,128)(2,1)} %get-tuple-element.90.back), channel_id=1, source_target_pairs={{0,1},{1,0},{2,3},{3,2},{4,5},{5,4},{6,7},{7,6},{8,9},{9,8},{10,11... | collective-permute-start | bytes 1277960 | tf_op jit(solution)/shard_map/ppermute | solution.py:34
  172.4 33.6 %collective-permute-start.35 = (bf16[208,1024]{1,0:T(8,128)(2,1)}, bf16[208,1024]{1,0:T(8,128)(2,1)}, u32[]{:S(2)}, u32[]{:S(2)}) collective-permute-start(bf16[208,1024]{1,0:T(8,128)(2,1)} %get-tuple-element.95.back), channel_id=1, source_target_pairs={{0,1},{1,0},{2,3},{3,2},{4,5},{5,4},{6,7},{7,6},{8,9},{9,8},{10,11... | collective-permute-start | bytes 1277960 | tf_op jit(solution)/shard_map/ppermute | solution.py:34
  179.1 10.3 %collective-permute-start.33 = (bf16[2,208,128]{2,1,0:T(8,128)(2,1)S(1)}, bf16[2,208,128]{2,1,0:T(8,128)(2,1)S(1)}, u32[]{:S(2)}, u32[]{:S(2)}) collective-permute-start(bf16[2,208,128]{2,1,0:T(8,128)(2,1)S(1)} %get-tuple-element.234), channel_id=1, source_target_pairs={{0,2},{2,4},{4,6},{6,0},{1,3},{3,5},{5,7},{7,1},{8,10},{10,12},{12... | collective-permute-start | bytes 319496 | tf_op jit(solution)/shard_map/ppermute | solution.py:30
  180.0 12.3 %collective-permute-start.32 = (bf16[2,208,128]{2,1,0:T(8,128)(2,1)S(1)}, bf16[2,208,128]{2,1,0:T(8,128)(2,1)S(1)}, u32[]{:S(2)}, u32[]{:S(2)}) collective-permute-start(bf16[2,208,128]{2,1,0:T(8,128)(2,1)S(1)} %get-tuple-element.235), channel_id=1, source_target_pairs={{0,4},{2,6},{4,0},{6,2},{1,5},{3,7},{5,1},{7,3},{8,12},{10,14},{12... | collective-permute-start | bytes 319496 | tf_op jit(solution)/shard_map/ppermute | solution.py:30
  182.7 9.6 %collective-permute-start.31 = (bf16[2,208,128]{2,1,0:T(8,128)(2,1)S(1)}, bf16[2,208,128]{2,1,0:T(8,128)(2,1)S(1)}, u32[]{:S(2)}, u32[]{:S(2)}) collective-permute-start(bf16[2,208,128]{2,1,0:T(8,128)(2,1)S(1)} %get-tuple-element.233), channel_id=1, source_target_pairs={{0,6},{2,0},{4,2},{6,4},{1,7},{3,1},{5,3},{7,5},{8,14},{10,8},{12,... | collective-permute-start | bytes 319496 | tf_op jit(solution)/shard_map/ppermute | solution.py:30
  189.4 91.9 %collective-permute-start.51 = (bf16[4,512,256]{2,1,0:T(8,128)(2,1)}, bf16[4,512,256]{2,1,0:T(8,128)(2,1)S(1)}, u32[]{:S(2)}, u32[]{:S(2)}) collective-permute-start(bf16[4,512,256]{2,1,0:T(8,128)(2,1)} %get-tuple-element.130), channel_id=1, source_target_pairs={{0,8},{8,0},{16,24},{24,16},{1,9},{9,1},{17,25},{25,17},{2,10},{10... | collective-permute-start | bytes 3145736 | tf_op jit(solution)/shard_map/ppermute | solution.py:39
  192.3 111.9 %collective-permute-start.50 = (bf16[4,512,256]{2,1,0:T(8,128)(2,1)}, bf16[4,512,256]{2,1,0:T(8,128)(2,1)}, u32[]{:S(2)}, u32[]{:S(2)}) collective-permute-start(bf16[4,512,256]{2,1,0:T(8,128)(2,1)} %get-tuple-element.128), channel_id=1, source_target_pairs={{0,8},{8,0},{16,24},{24,16},{1,9},{9,1},{17,25},{25,17},{2,10},{10... | collective-permute-start | bytes 3145736 | tf_op jit(solution)/shard_map/ppermute | solution.py:39
  192.4 93.1 %collective-permute-start.57 = (bf16[4,512,256]{2,1,0:T(8,128)(2,1)}, bf16[4,512,256]{2,1,0:T(8,128)(2,1)S(1)}, u32[]{:S(2)}, u32[]{:S(2)}) collective-permute-start(bf16[4,512,256]{2,1,0:T(8,128)(2,1)} %get-tuple-element.136), channel_id=1, source_target_pairs={{0,8},{8,0},{16,24},{24,16},{1,9},{9,1},{17,25},{25,17},{2,10},{10... | collective-permute-start | bytes 3145736 | tf_op jit(solution)/shard_map/ppermute | solution.py:39
  204.7 13.5 %collective-permute-start.36 = (bf16[208,1024]{1,0:T(8,128)(2,1)}, bf16[208,1024]{1,0:T(8,128)(2,1)S(1)}, u32[]{:S(2)}, u32[]{:S(2)}) collective-permute-start(bf16[208,1024]{1,0:T(8,128)(2,1)} %get-tuple-element.93.refs_2_), channel_id=1, source_target_pairs={{0,1},{1,0},{2,3},{3,2},{4,5},{5,4},{6,7},{7,6},{8,9},{9,8},{10,11... | collective-permute-start | bytes 1277960 | tf_op jit(solution)/shard_map/ppermute | solution.py:34
  216.1 11.3 %collective-permute-start.37 = (bf16[208,1024]{1,0:T(8,128)(2,1)}, bf16[208,1024]{1,0:T(8,128)(2,1)S(1)}, u32[]{:S(2)}, u32[]{:S(2)}) collective-permute-start(bf16[208,1024]{1,0:T(8,128)(2,1)} %get-tuple-element.98.refs_3_), channel_id=1, source_target_pairs={{0,1},{1,0},{2,3},{3,2},{4,5},{5,4},{6,7},{7,6},{8,9},{9,8},{10,11... | collective-permute-start | bytes 1277960 | tf_op jit(solution)/shard_map/ppermute | solution.py:34
  244.9 54.3 %collective-permute-start.42 = (bf16[4,512,256]{2,1,0:T(8,128)(2,1)}, bf16[4,512,256]{2,1,0:T(8,128)(2,1)}, u32[]{:S(2)}, u32[]{:S(2)}) collective-permute-start(bf16[4,512,256]{2,1,0:T(8,128)(2,1)} %get-tuple-element.113), channel_id=1, source_target_pairs={{0,8},{8,0},{16,24},{24,16},{1,9},{9,1},{17,25},{25,17},{2,10},{10... | collective-permute-start | bytes 3145736 | tf_op jit(solution)/shard_map/ppermute | solution.py:39
  245.6 38.7 %collective-permute-start.40 = (bf16[2,208,128]{2,1,0:T(8,128)(2,1)}, bf16[2,208,128]{2,1,0:T(8,128)(2,1)}, u32[]{:S(2)}, u32[]{:S(2)}) collective-permute-start(bf16[2,208,128]{2,1,0:T(8,128)(2,1)} %get-tuple-element.229), channel_id=1, source_target_pairs={{0,2},{2,4},{4,6},{6,0},{1,3},{3,5},{5,7},{7,1},{8,10},{10,12},{12... | collective-permute-start | bytes 319496 | tf_op jit(solution)/shard_map/ppermute | solution.py:30
  282.6 22.8 %collective-permute-start.52 = (bf16[4,512,256]{2,1,0:T(8,128)(2,1)}, bf16[4,512,256]{2,1,0:T(8,128)(2,1)}, u32[]{:S(2)}, u32[]{:S(2)}) collective-permute-start(bf16[4,512,256]{2,1,0:T(8,128)(2,1)} %add_convert_fusion.4), channel_id=1, source_target_pairs={{0,16},{8,24},{16,0},{24,8},{1,17},{9,25},{17,1},{25,9},{2,18},{10... | collective-permute-start | bytes 3145736 | tf_op jit(solution)/shard_map/ppermute | solution.py:39
  288.8 19.3 %collective-permute-start.56 = (bf16[4,512,256]{2,1,0:T(8,128)(2,1)}, bf16[4,512,256]{2,1,0:T(8,128)(2,1)}, u32[]{:S(2)}, u32[]{:S(2)}) collective-permute-start(bf16[4,512,256]{2,1,0:T(8,128)(2,1)} %get-tuple-element.134), channel_id=1, source_target_pairs={{0,8},{8,0},{16,24},{24,16},{1,9},{9,1},{17,25},{25,17},{2,10},{10... | collective-permute-start | bytes 3145736 | tf_op jit(solution)/shard_map/ppermute | solution.py:39
  293.6 33.2 %collective-permute-start.58 = (bf16[4,512,256]{2,1,0:T(8,128)(2,1)S(1)}, bf16[4,512,256]{2,1,0:T(8,128)(2,1)}, u32[]{:S(2)}, u32[]{:S(2)}) collective-permute-start(bf16[4,512,256]{2,1,0:T(8,128)(2,1)S(1)} %add_convert_fusion.1), channel_id=1, source_target_pairs={{0,16},{8,24},{16,0},{24,8},{1,17},{9,25},{17,1},{25,9},{2,18},{10... | collective-permute-start | bytes 3145736 | tf_op jit(solution)/shard_map/ppermute | solution.py:39
  299.2 60.2 %collective-permute-start.41 = (bf16[4,512,256]{2,1,0:T(8,128)(2,1)}, bf16[4,512,256]{2,1,0:T(8,128)(2,1)S(1)}, u32[]{:S(2)}, u32[]{:S(2)}) collective-permute-start(bf16[4,512,256]{2,1,0:T(8,128)(2,1)} %get-tuple-element.111), channel_id=1, source_target_pairs={{0,8},{8,0},{16,24},{24,16},{1,9},{9,1},{17,25},{25,17},{2,10},{10... | collective-permute-start | bytes 3145736 | tf_op jit(solution)/shard_map/ppermute | solution.py:39
  304.2 55.3 %collective-permute-start.43 = (bf16[4,512,256]{2,1,0:T(8,128)(2,1)S(1)}, bf16[4,512,256]{2,1,0:T(8,128)(2,1)S(1)}, u32[]{:S(2)}, u32[]{:S(2)}) collective-permute-start(bf16[4,512,256]{2,1,0:T(8,128)(2,1)S(1)} %add_convert_fusion.7), channel_id=1, source_target_pairs={{0,16},{8,24},{16,0},{24,8},{1,17},{9,25},{17,1},{25,9},{2,18},{10... | collective-permute-start | bytes 3145736 | tf_op jit(solution)/shard_map/ppermute | solution.py:39
  307.5 23.5 %collective-permute-start.55 = (bf16[512,256]{1,0:T(8,128)(2,1)S(1)}, bf16[512,256]{1,0:T(8,128)(2,1)S(1)}, u32[]{:S(2)}, u32[]{:S(2)}) collective-permute-start(bf16[512,256]{1,0:T(8,128)(2,1)S(1)} %get-tuple-element.209), channel_id=1, source_target_pairs={{0,2},{2,4},{4,6},{6,0},{1,3},{3,5},{5,7},{7,1},{8,10},{10,12},{12... | collective-permute-start | bytes 786440 | tf_op jit(solution)/shard_map/ppermute | solution.py:30
  308.1 22.9 %collective-permute-start.54 = (bf16[512,256]{1,0:T(8,128)(2,1)S(1)}, bf16[512,256]{1,0:T(8,128)(2,1)S(1)}, u32[]{:S(2)}, u32[]{:S(2)}) collective-permute-start(bf16[512,256]{1,0:T(8,128)(2,1)S(1)} %get-tuple-element.210), channel_id=1, source_target_pairs={{0,4},{2,6},{4,0},{6,2},{1,5},{3,7},{5,1},{7,3},{8,12},{10,14},{12... | collective-permute-start | bytes 786440 | tf_op jit(solution)/shard_map/ppermute | solution.py:30
  331.1 22.6 %collective-permute-start.60 = (bf16[512,256]{1,0:T(8,128)(2,1)S(1)}, bf16[512,256]{1,0:T(8,128)(2,1)S(1)}, u32[]{:S(2)}, u32[]{:S(2)}) collective-permute-start(bf16[512,256]{1,0:T(8,128)(2,1)S(1)} %get-tuple-element.207), channel_id=1, source_target_pairs={{0,4},{2,6},{4,0},{6,2},{1,5},{3,7},{5,1},{7,3},{8,12},{10,14},{12... | collective-permute-start | bytes 786440 | tf_op jit(solution)/shard_map/ppermute | solution.py:30
  333.2 23.3 %collective-permute-start.59 = (bf16[512,256]{1,0:T(8,128)(2,1)S(1)}, bf16[512,256]{1,0:T(8,128)(2,1)S(1)}, u32[]{:S(2)}, u32[]{:S(2)}) collective-permute-start(bf16[512,256]{1,0:T(8,128)(2,1)S(1)} %get-tuple-element.205), channel_id=1, source_target_pairs={{0,6},{2,0},{4,2},{6,4},{1,7},{3,1},{5,3},{7,5},{8,14},{10,8},{12,... | collective-permute-start | bytes 786440 | tf_op jit(solution)/shard_map/ppermute | solution.py:30
  360.5 19.0 %collective-permute-start.45 = (bf16[512,256]{1,0:T(8,128)(2,1)S(1)}, bf16[512,256]{1,0:T(8,128)(2,1)S(1)}, u32[]{:S(2)}, u32[]{:S(2)}) collective-permute-start(bf16[512,256]{1,0:T(8,128)(2,1)S(1)} %get-tuple-element.213), channel_id=1, source_target_pairs={{0,4},{2,6},{4,0},{6,2},{1,5},{3,7},{5,1},{7,3},{8,12},{10,14},{12... | collective-permute-start | bytes 786440 | tf_op jit(solution)/shard_map/ppermute | solution.py:30
  360.6 23.5 %collective-permute-start.44 = (bf16[512,256]{1,0:T(8,128)(2,1)S(1)}, bf16[512,256]{1,0:T(8,128)(2,1)S(1)}, u32[]{:S(2)}, u32[]{:S(2)}) collective-permute-start(bf16[512,256]{1,0:T(8,128)(2,1)S(1)} %get-tuple-element.211), channel_id=1, source_target_pairs={{0,6},{2,0},{4,2},{6,4},{1,7},{3,1},{5,3},{7,5},{8,14},{10,8},{12,... | collective-permute-start | bytes 786440 | tf_op jit(solution)/shard_map/ppermute | solution.py:30
  (71 other events, 607.0 us)
